TPU v7x, 32 devices: a whole 2x2x4 slice. The times are simulated.
32 devices in a mesh: height: 16 (over z, x, core), plan: 2 (over y).
Axes of the slice: x: 2, y: 2, z: 4, core: 2. Of those that a mesh axis runs over, the one named last changes fastest.
Arguments:
- displacement: float32 [3, 16, 40, 256], P(None, 'height', None, 'plan'), may hold values from -3 to 3
- velocity: float32 [3, 16, 40, 256], P(None, 'height', None, 'plan'), may hold values from -3 to 3
- lumped_mass: float32 [16, 40, 256], P('height', None, 'plan'), may hold values from 0.3 to 3
- plastic_strain: float32 [3, 8, 16, 40, 256], P(None, None, 'height', None, 'plan'), may hold values from -1 to 1
- hardening_strain: float32 [3, 8, 16, 40, 256], P(None, None, 'height', None, 'plan'), may hold values from 0.01 to 0.5
- material_ids: int32 [3, 8, 16, 40, 256], P(None, None, 'height', None, 'plan'), may hold values from 0 to 7
- material_table: float32 [8, 3], replicated, may hold values from 0.5 to 2
- ground_accel: float32 [4, 3], replicated, may hold values from -4 to 4
- snapshot_history: bfloat16 [60, 3, 16, 40, 256], P(None, None, 'height', None, 'plan'), may hold values from -6 to 6
- mode_shapes: bfloat16 [256, 3, 16, 40, 256], P(None, None, 'height', None, 'plan'), as said below
Outputs:
- displacement_end: float32 [3, 16, 40, 256], P(None, 'height', None, 'plan')
- velocity_end: float32 [3, 16, 40, 256], P(None, 'height', None, 'plan')
- plastic_end: float32 [3, 8, 16, 40, 256], P(None, None, 'height', None, 'plan')
- hardening_end: float32 [3, 8, 16, 40, 256], P(None, None, 'height', None, 'plan')
- modal_coords: float32 [256, 64], P(('height', 'plan'))
Inputs may be any that keep to these rules, and one draw needn't show every extreme that they name: mode_shapes are scaled so that mass_gram is positive definite and well conditioned.
All inputs are finite; a program needn't handle non-finite values.
Results may differ from a plain program's by a relative error of at most 0.0083.
Values sent between devices are 32-bit elements; how exact they have to be, the bound alone decides.
A program may use at most 128 MiB of HBM per device.

v0:
```python
import jax
import jax.numpy as jnp
from jax import lax
from jax.sharding import PartitionSpec as P

time_step = 0.3
mass_damping = 0.1
stiff_damping = 0.05
shear_stiff = 0.5
axial_components = (2, 1, 0)


def passed_along(block, axis, distance):
    devices = range(lax.axis_size(axis))
    route = [(i - distance, i) for i in devices if i - distance in devices]
    return lax.ppermute(block, axis, route)


def from_behind(block, axis, distance):
    devices = range(lax.axis_size(axis))
    route = [((i - distance) % len(devices), i) for i in devices]
    return lax.ppermute(block, axis, route)


def fibre_props(material_ids, material_table):
    modulus = jnp.zeros(material_ids.shape, jnp.float32)
    yields = jnp.zeros(material_ids.shape, jnp.float32)
    slopes = jnp.zeros(material_ids.shape, jnp.float32)
    for material_index in range(material_table.shape[0]):
        selected = (material_ids == material_index).astype(jnp.float32)
        modulus = modulus + selected * material_table[material_index, 0]
        yields = yields + selected * (0.4 * material_table[material_index, 1])
        slopes = slopes + selected * (0.1 * material_table[material_index, 2])
    return (modulus, yields, slopes)


def bar_update(stretch, stretch_rate, plastic, harden, modulus, yields, slopes, axial_index):
    trial_stress = modulus * (stretch[axial_index][None] - plastic)
    excess = jnp.abs(trial_stress) - (yields + slopes * harden)
    growth = jnp.maximum(excess, 0.0) / (modulus + slopes)
    flow_sign = jnp.sign(trial_stress)
    plastic_new = plastic + growth * flow_sign
    harden_new = harden + growth
    stress = trial_stress - modulus * growth * flow_sign
    axial_force = jnp.mean(stress, axis=0)
    tangent = jnp.mean(modulus, axis=0)
    component_list = []
    for component in range(3):
        if component == axial_index:
            component_list.append(axial_force + stiff_damping * tangent * stretch_rate[component])
        else:
            component_list.append(
                shear_stiff * (stretch[component] + stiff_damping * stretch_rate[component])
            )
    return (jnp.stack(component_list), plastic_new, harden_new)


def earlier_fields(field, below_rim, left_rim):
    along_height = jnp.concatenate([below_rim, field[:, :-1]], axis=1)
    along_rows = jnp.concatenate([jnp.zeros_like(field[:, :, :1]), field[:, :, :-1]], axis=2)
    along_rim = jnp.concatenate([left_rim, field[:, :, :, :-1]], axis=3)
    return (along_height, along_rows, along_rim)


def body(
    displacement,
    velocity,
    lumped_mass,
    plastic_strain,
    hardening_strain,
    material_ids,
    material_table,
    ground_accel,
    snapshot_history,
    mode_shapes,
):
    modulus, yields, slopes = fibre_props(material_ids, material_table)
    disp_now, velo_now = (displacement, velocity)
    plastic_now, harden_now = (plastic_strain, hardening_strain)
    new_snapshots = []
    for step_index in range(ground_accel.shape[0]):
        below_disp, below_velo = passed_along((disp_now, velo_now), "height", 1)
        left_disp, left_velo = from_behind(
            (disp_now[:, :, :, -1:], velo_now[:, :, :, -1:]), "plan", 1
        )
        earlier_disp = earlier_fields(disp_now, below_disp, left_disp)
        earlier_velo = earlier_fields(velo_now, below_velo, left_velo)
        bar_forces, plastic_parts, harden_parts = ([], [], [])
        for bar_index in range(3):
            bar_force, plastic_part, harden_part = bar_update(
                disp_now - earlier_disp[bar_index],
                velo_now - earlier_velo[bar_index],
                plastic_now[bar_index],
                harden_now[bar_index],
                modulus[bar_index],
                yields[bar_index],
                slopes[bar_index],
                axial_components[bar_index],
            )
            bar_forces.append(bar_force)
            plastic_parts.append(plastic_part)
            harden_parts.append(harden_part)
        above_force = passed_along(bar_forces[0], "height", -1)
        plastic_now = jnp.stack(plastic_parts)
        harden_now = jnp.stack(harden_parts)
        right_force = from_behind(bar_forces[2][:, :, :, :1], "plan", -1)
        later_height = jnp.concatenate([bar_forces[0][:, 1:], above_force], axis=1)
        later_rows = jnp.concatenate(
            [bar_forces[1][:, :, 1:], jnp.zeros_like(bar_forces[1][:, :, :1])], axis=2
        )
        later_rim = jnp.concatenate([bar_forces[2][:, :, :, 1:], right_force], axis=3)
        resisting = (
            bar_forces[0]
            - later_height
            + (bar_forces[1] - later_rows)
            + (bar_forces[2] - later_rim)
        )
        acceleration = (
            -ground_accel[step_index][:, None, None, None] - resisting / lumped_mass[None]
        )
        velo_now = (
            (1.0 - 0.5 * mass_damping * time_step) * velo_now + time_step * acceleration
        ) / (1.0 + 0.5 * mass_damping * time_step)
        disp_now = disp_now + time_step * velo_now
        new_snapshots.append(disp_now.astype(jnp.bfloat16))
    snapshots = jnp.concatenate([snapshot_history, jnp.stack(new_snapshots)], axis=0)
    mode_count = mode_shapes.shape[0]
    flat_modes = mode_shapes.reshape(mode_count, -1)
    weighted = (
        (mode_shapes.astype(jnp.float32) * lumped_mass[None, None])
        .astype(jnp.bfloat16)
        .reshape(mode_count, -1)
    )
    flat_snaps = snapshots.reshape(snapshots.shape[0], -1)
    contract_last = (((1,), (1,)), ((), ()))
    mass_gram = lax.dot_general(
        weighted, flat_modes, contract_last, preferred_element_type=jnp.float32
    )
    projected = lax.dot_general(
        weighted, flat_snaps, contract_last, preferred_element_type=jnp.float32
    )
    devices_all = lax.axis_size(("height", "plan"))
    row_count = mode_count // devices_all
    gram_total, projected_total = lax.psum((mass_gram, projected), ("height", "plan"))
    factor = jnp.linalg.cholesky(gram_total)
    coords_all = jax.scipy.linalg.cho_solve((factor, True), projected_total)
    modal_coords = lax.dynamic_slice_in_dim(
        coords_all, lax.axis_index(("height", "plan")) * row_count, row_count, 0
    )
    return (disp_now, velo_now, plastic_now, harden_now, modal_coords)


def solution(mesh):
    return jax.shard_map(
        body,
        mesh=mesh,
        in_specs=(
            P(None, "height", None, "plan"),
            P(None, "height", None, "plan"),
            P("height", None, "plan"),
            P(None, None, "height", None, "plan"),
            P(None, None, "height", None, "plan"),
            P(None, None, "height", None, "plan"),
            P(),
            P(),
            P(None, None, "height", None, "plan"),
            P(None, None, "height", None, "plan"),
        ),
        out_specs=(
            P(None, "height", None, "plan"),
            P(None, "height", None, "plan"),
            P(None, None, "height", None, "plan"),
            P(None, None, "height", None, "plan"),
            P(("height", "plan"), None),
        ),
        check_vma=False,
    )
```

profile of v0, /device:TPU:0, one launch (start us, length us, event | category | flops | bytes accessed | tf_op | source)
XLA Modules:
  0.0 343.2 jit_solution(6548634647187151271)
XLA Ops:
  7.2 2.4 collective-permute-start.1
  10.5 2.4 collective-permute-start.4
  12.9 3.4 collective-permute-start
  19.9 2.1 fusion.259
  33.3 6.5 %select_add_fusion.2 = (f32[3,8,1,40,128]{4,3,1,2,0:T(8,128)S(1)}, pred[3,8,1,40,128]{4,3,1,2,0:T(8,128)(4,1)S(1)}, pred[3,8,1,40,128]{4,3,1,2,0:T(8,128)(4,1)S(...) fusion(f32[]{:T(128)} %bitcast.22, f32[]{:T(128)} %bitcast.20, ...), kind=kLoop, calls=%fused_computation.32 | loop fusion | flops 2826240 | bytes 1966112 | tf_op jit(solution)/shard_map/add | solution.py:31
  39.9 7.8 %fusion = bf16[256,3,40,128]{3,2,1,0:T(8,128)(2,1)} fusion(bf16[256,3,1,40,128]{4,3,2,1,0:T(8,128)(2,1)} %param.19, f32[40,128]{1,0:T(8,128)} %bitcast.1505), kind=kLoop, calls=%fused_computation.3 | loop fusion | flops 11796480 | bytes 15749120 | tf_op jit(solution)/shard_map/reshape.979
  47.7 8.4 %fusion.7 = f32[256,256]{0,1:T(8,128)} fusion(bf16[256,3,40,128]{3,2,1,0:T(8,128)(2,1)} %bitcast.1489, bf16[256,3,40,128]{3,2,1,0:T(8,128)(2,1)} %fusion), kind=kOutput, calls=%fused_computation.10 | convolution fusion | flops 2013265920 | bytes 15990784 | tf_op jit(solution)/shard_map/dot_general | solution.py:136
  57.1 3.4 copy.614
  64.0 1.6 collective-permute-start.5
  65.7 3.1 collective-permute-done.5
  70.5 1.7 collective-permute-start.6
  72.9 3.8 %collective-permute-start.7 = (f32[3,1,40,128]{3,2,1,0:T(8,128)S(1)}, f32[3,1,40,128]{3,2,1,0:T(8,128)S(1)}, u32[]{:S(2)}, u32[]{:S(2)}) collective-permute-start(f32[3,1,40,128]{3,2,1,0:T(8,128)S(1)} %get-tuple-element.141), channel_id=1, source_target_pairs={{0,2},{2,4},{4,6},{6,8},{8,10},{10,12},{12,14},{14,16},{16,18},{18... | collective-permute-start | bytes 184328 | tf_op jit(solution)/shard_map/ppermute | solution.py:16
  79.5 1.6 collective-permute-start.11
  81.2 3.0 collective-permute-done.11
  84.4 2.7 collective-permute-start.13
  90.0 4.3 %collective-permute-start.12 = (f32[3,1,40,128]{3,2,0,1:T(8,128)S(1)}, f32[3,1,40,128]{3,2,0,1:T(8,128)S(1)}, u32[]{:S(2)}, u32[]{:S(2)}) collective-permute-start(f32[3,1,40,128]{3,2,0,1:T(8,128)S(1)} %get-tuple-element.63), channel_id=1, source_target_pairs={{0,2},{2,4},{4,6},{6,8},{8,10},{10,12},{12,14},{14,16},{16,18},{18... | collective-permute-start | bytes 184328 | tf_op jit(solution)/shard_map/ppermute | solution.py:16
  95.8 3.4 collective-permute-done.15
  102.3 4.1 %collective-permute-done.17 = f32[3,1,40,1]{3,2,0,1:T(8,128)S(1)} collective-permute-done((f32[3,1,40,1]{3,2,0,1:T(8,128)S(1)}, f32[3,1,40,1]{3,2,0,1:T(8,128)S(1)}, u32[]{:S(2)}, u32[]{:S(2)}) %collective-permute-start.17) | collective-permute-done | bytes 512 | tf_op jit(solution)/shard_map/ppermute | solution.py:22
  107.2 2.3 collective-permute-start.19
  109.6 4.7 %collective-permute-start.18 = (f32[3,1,40,128]{3,2,0,1:T(8,128)S(1)}, f32[3,1,40,128]{3,2,0,1:T(8,128)S(1)}, u32[]{:S(2)}, u32[]{:S(2)}) collective-permute-start(f32[3,1,40,128]{3,2,0,1:T(8,128)S(1)} %get-tuple-element.60), channel_id=1, source_target_pairs={{0,2},{2,4},{4,6},{6,8},{8,10},{10,12},{12,14},{14,16},{16,18},{18... | collective-permute-start | bytes 184328 | tf_op jit(solution)/shard_map/ppermute | solution.py:16
  114.9 1.6 collective-permute-start.21
  116.5 2.4 collective-permute-done.22
  127.1 8.1 %concatenate.169 = bf16[64,3,1,40,128]{4,0,3,1,2:T(8,128)(2,1)S(1)} concatenate(bf16[60,3,1,40,128]{4,0,3,1,2:T(8,128)(2,1)} %copy.614, bf16[1,3,1,40,128]{4,0,3,1,2:T(2,128)(2,1)S(1)} %copy.615, bf16[1,3,1,40,128]{4,0,3,1,2:T(2,128)(2,1)S(1)} %copy.616, bf16[1,3,1,40,128]{4,0,3,1,2:T(2,128)(2,1)S(1)} %copy.617, bf16[1,3,1,40,128]{4,0,3,1,2:T(2,128)(2,1)S(1)} %copy.618), dimensions={0} | concatenate | bytes 3932160 | tf_op jit(solution)/shard_map/concatenate | solution.py:126
  135.2 6.3 %fusion.12 = f32[256,64]{0,1:T(8,128)} fusion(bf16[64,3,1,40,128]{4,0,3,1,2:T(8,128)(2,1)S(1)} %concatenate.169, bf16[256,3,40,128]{3,2,1,0:T(8,128)(2,1)} %fusion), kind=kOutput, calls=%fused_computation.11 | convolution fusion | flops 503316480 | bytes 9895936 | tf_op jit(solution)/shard_map/dot_general | solution.py:139
  142.3 126.1 %all-reduce.16.cloned.1.call-done = (f32[256,256]{0,1:T(8,128)}, f32[256,64]{0,1:T(8,128)}) async-done(((f32[256,256]{0,1:T(8,128)}, f32[256,64]{0,1:T(8,128)}), (f32[256,256]{0,1:T(8,128)}, f32[256,64]{0,1:T(8,128)})) %all-reduce.16.cloned.1.call-update) | async-done | bytes 327696 | tf_op jit(solution)/shard_map/psum | solution.py:144
  270.4 11.7 %cholesky.50 = f32[128,128]{1,0:T(8,128)S(1)} custom-call(f32[128,128]{1,0:T(8,128)S(1)} %cholesky.118), custom_call_target="Cholesky" | custom-call | tf_op jit(solution)/shard_map/jit(cholesky)/cholesky | solution.py:145
  282.8 9.8 %custom-call.18 = f32[1,128,128]{1,2,0:T(8,128)S(1)} custom-call(f32[1,128,128]{2,1,0:T(8,128)S(1)} %get-tuple-element.114), custom_call_target="InvertDiagBlocksLowerTriangular" | custom-call | tf_op jit(solution)/shard_map/jit(cholesky)/cholesky | solution.py:145
  293.1 11.7 %cholesky.105 = f32[128,128]{1,0:T(8,128)S(1)} custom-call(f32[128,128]{1,0:T(8,128)S(1)} %convolution_subtract_fusion), custom_call_target="Cholesky" | custom-call | tf_op jit(solution)/shard_map/jit(cholesky)/cholesky | solution.py:145
  306.9 5.3 %while.1 = (s32[]{:T(128)}, f32[256,256]{1,0:T(8,128)S(1)}, s32[2,2]{1,0:T(2,128)S(1)}, f32[2,128,128]{2,1,0:T(8,128)}, s32[]{:T(128)}) while((s32[]{:T(128)}, f32[256,256]{1,0:T(8,128)S(1)}, s32[2,2]{1,0:T(2,128)S(1)}, f32[2,128,128]{2,1,0:T(8,128)}, s32[]{:T(128)}) %tuple.124), condition=%wide.while_cond, body=%wide.while_body.sunk | while | flops 2 | bytes 132205 | solution.py:146
  307.7 2.0 bitcast_dynamic-update-slice_fusion.2
  310.3 2.0 bitcast_dynamic-update-slice_fusion.2
  312.3 20.5 %custom-call.19 = f32[2,128,128]{1,2,0:T(8,128)S(1)} custom-call(f32[2,128,128]{2,1,0:T(8,128)} %get-tuple-element.12), custom_call_target="InvertDiagBlocksLowerTriangular" | custom-call | tf_op jit(solution)/shard_map/jit(_cho_solve)/triangular_solve | solution.py:146
  (174 shorter events, 42.1 us)
Async XLA Ops:
  7.2 261.2 %all-reduce.16.cloned.1.call-start = ((), (), s32[]{:S(2)}) async-start(), calls=%async_computation | async-start | bytes 655360 | tf_op jit(solution)/shard_map/psum | solution.py:144
  7.2 54.9 %collective-permute-start.1 = (f32[3,1,40,128]{3,2,1,0:T(8,128)}, f32[3,1,40,128]{3,2,1,0:T(8,128)S(1)}, u32[]{:S(2)}, u32[]{:S(2)}) collective-permute-start(f32[3,1,40,128]{3,2,1,0:T(8,128)} %param.11), channel_id=1, source_target_pairs={{0,2},{2,4},{4,6},{6,8},{8,10},{10,12},{12,14},{14,16},{16,18},{18... | collective-permute-start | bytes 184328 | tf_op jit(solution)/shard_map/ppermute | solution.py:16
  10.5 51.6 %collective-permute-start.4 = (f32[3,1,40,1]{3,2,1,0:T(8,128)S(1)}, f32[3,1,40,1]{3,2,1,0:T(8,128)S(1)}, u32[]{:S(2)}, u32[]{:S(2)}) collective-permute-start(f32[3,1,40,1]{3,2,1,0:T(8,128)S(1)} %slice.600), channel_id=1, source_target_pairs={{1,0},{0,1},{3,2},{2,3},{5,4},{4,5},{7,6},{6,7},{9,8},{8,9},{11,10... | collective-permute-start | bytes 1448 | tf_op jit(solution)/shard_map/ppermute | solution.py:22
  12.9 47.6 %collective-permute-start = (f32[3,1,40,128]{3,2,1,0:T(8,128)}, f32[3,1,40,128]{3,2,1,0:T(8,128)S(1)}, u32[]{:S(2)}, u32[]{:S(2)}) collective-permute-start(f32[3,1,40,128]{3,2,1,0:T(8,128)} %param.10), channel_id=1, source_target_pairs={{0,2},{2,4},{4,6},{6,8},{8,10},{10,12},{12,14},{14,16},{16,18},{18... | collective-permute-start | bytes 184328 | tf_op jit(solution)/shard_map/ppermute | solution.py:16
  17.8 42.7 %collective-permute-start.3 = (f32[3,1,40,1]{3,2,1,0:T(8,128)}, f32[3,1,40,1]{3,2,1,0:T(8,128)S(1)}, u32[]{:S(2)}, u32[]{:S(2)}) collective-permute-start(f32[3,1,40,1]{3,2,1,0:T(8,128)} %slice.593), channel_id=1, source_target_pairs={{1,0},{0,1},{3,2},{2,3},{5,4},{4,5},{7,6},{6,7},{9,8},{8,9},{11,10... | collective-permute-start | bytes 1448 | tf_op jit(solution)/shard_map/ppermute | solution.py:22
  47.7 13.5 %copy-start.2 = (f32[3,1,40,128]{3,2,1,0:T(8,128)S(1)}, f32[3,1,40,128]{3,2,1,0:T(8,128)}, u32[]{:S(2)}) copy-start(f32[3,1,40,128]{3,2,1,0:T(8,128)} %param.10) | copy-start | bytes 184324
  47.7 14.4 %copy-start.3 = (f32[3,1,40,128]{3,2,1,0:T(8,128)S(1)}, f32[3,1,40,128]{3,2,1,0:T(8,128)}, u32[]{:S(2)}) copy-start(f32[3,1,40,128]{3,2,1,0:T(8,128)} %param.11) | copy-start | bytes 184324
  56.1 6.1 %copy-start = (f32[3,8,1,40,128]{4,3,2,1,0:T(8,128)S(1)}, f32[3,8,1,40,128]{4,3,2,1,0:T(8,128)}, u32[]{:S(2)}) copy-start(f32[3,8,1,40,128]{4,3,2,1,0:T(8,128)} %param.14) | copy-start | bytes 1474564
  56.1 6.1 %copy-start.1 = (f32[3,8,1,40,128]{4,3,2,1,0:T(8,128)S(1)}, f32[3,8,1,40,128]{4,3,2,1,0:T(8,128)}, u32[]{:S(2)}) copy-start(f32[3,8,1,40,128]{4,3,2,1,0:T(8,128)} %param.13) | copy-start | bytes 1474564
  56.1 12.7 %copy-start.4 = (f32[1,40,128]{2,1,0:T(8,128)S(1)}, f32[1,40,128]{2,1,0:T(8,128)}, u32[]{:S(2)}) copy-start(f32[1,40,128]{2,1,0:T(8,128)} %param.12) | copy-start | bytes 61444
  62.6 6.1 %collective-permute-start.2 = (f32[3,1,40,128]{3,2,1,0:T(8,128)S(1)}, f32[3,1,40,128]{3,2,1,0:T(8,128)S(1)}, u32[]{:S(2)}, u32[]{:S(2)}) collective-permute-start(f32[3,1,40,128]{3,2,1,0:T(8,128)S(1)} %pad_maximum_fusion.2), channel_id=1, source_target_pairs={{2,0},{4,2},{6,4},{8,6},{10,8},{12,10},{14,12},{16,14},{18,16},{20... | collective-permute-start | bytes 184328 | tf_op jit(solution)/shard_map/ppermute | solution.py:16
  64.0 4.8 %collective-permute-start.5 = (f32[3,1,40,1]{3,2,0,1:T(8,128)S(1)}, f32[3,1,40,1]{3,2,0,1:T(8,128)S(1)}, u32[]{:S(2)}, u32[]{:S(2)}) collective-permute-start(f32[3,1,40,1]{3,2,0,1:T(8,128)S(1)} %bitcast.1515), channel_id=1, source_target_pairs={{1,0},{0,1},{3,2},{2,3},{5,4},{4,5},{7,6},{6,7},{9,8},{8,9},{11,10... | collective-permute-start | bytes 1448 | tf_op jit(solution)/shard_map/ppermute | solution.py:22
  68.9 7.7 %collective-permute-start.9 = (f32[3,1,40,1]{3,2,0,1:T(8,128)S(1)}, f32[3,1,40,1]{3,2,0,1:T(8,128)S(1)}, u32[]{:S(2)}, u32[]{:S(2)}) collective-permute-start(f32[3,1,40,1]{3,2,0,1:T(8,128)S(1)} %slice.754), channel_id=1, source_target_pairs={{1,0},{0,1},{3,2},{2,3},{5,4},{4,5},{7,6},{6,7},{9,8},{8,9},{11,10... | collective-permute-start | bytes 1448 | tf_op jit(solution)/shard_map/ppermute | solution.py:22
  70.5 6.4 %collective-permute-start.6 = (f32[3,1,40,128]{3,2,1,0:T(8,128)S(1)}, f32[3,1,40,128]{3,2,1,0:T(8,128)S(1)}, u32[]{:S(2)}, u32[]{:S(2)}) collective-permute-start(f32[3,1,40,128]{3,2,1,0:T(8,128)S(1)} %bitcast.1492), channel_id=1, source_target_pairs={{0,2},{2,4},{4,6},{6,8},{8,10},{10,12},{12,14},{14,16},{16,18},{18... | collective-permute-start | bytes 184328 | tf_op jit(solution)/shard_map/ppermute | solution.py:16
  72.3 4.4 %collective-permute-start.10 = (f32[3,1,40,1]{3,2,0,1:T(8,128)S(1)}, f32[3,1,40,1]{3,2,0,1:T(8,128)S(1)}, u32[]{:S(2)}, u32[]{:S(2)}) collective-permute-start(f32[3,1,40,1]{3,2,0,1:T(8,128)S(1)} %slice.757), channel_id=1, source_target_pairs={{1,0},{0,1},{3,2},{2,3},{5,4},{4,5},{7,6},{6,7},{9,8},{8,9},{11,10... | collective-permute-start | bytes 1448 | tf_op jit(solution)/shard_map/ppermute | solution.py:22
  72.9 4.7 %collective-permute-start.7 = (f32[3,1,40,128]{3,2,1,0:T(8,128)S(1)}, f32[3,1,40,128]{3,2,1,0:T(8,128)S(1)}, u32[]{:S(2)}, u32[]{:S(2)}) collective-permute-start(f32[3,1,40,128]{3,2,1,0:T(8,128)S(1)} %get-tuple-element.141), channel_id=1, source_target_pairs={{0,2},{2,4},{4,6},{6,8},{8,10},{10,12},{12,14},{14,16},{16,18},{18... | collective-permute-start | bytes 184328 | tf_op jit(solution)/shard_map/ppermute | solution.py:16
  78.2 6.0 %collective-permute-start.8 = (f32[3,1,40,128]{3,2,1,0:T(8,128)S(1)}, f32[3,1,40,128]{3,2,1,0:T(8,128)S(1)}, u32[]{:S(2)}, u32[]{:S(2)}) collective-permute-start(f32[3,1,40,128]{3,2,1,0:T(8,128)S(1)} %pad_maximum_fusion.5), channel_id=1, source_target_pairs={{2,0},{4,2},{6,4},{8,6},{10,8},{12,10},{14,12},{16,14},{18,16},{20... | collective-permute-start | bytes 184328 | tf_op jit(solution)/shard_map/ppermute | solution.py:16
  79.5 4.7 %collective-permute-start.11 = (f32[3,1,40,1]{3,2,0,1:T(8,128)S(1)}, f32[3,1,40,1]{3,2,0,1:T(8,128)S(1)}, u32[]{:S(2)}, u32[]{:S(2)}) collective-permute-start(f32[3,1,40,1]{3,2,0,1:T(8,128)S(1)} %bitcast.1516), channel_id=1, source_target_pairs={{1,0},{0,1},{3,2},{2,3},{5,4},{4,5},{7,6},{6,7},{9,8},{8,9},{11,10... | collective-permute-start | bytes 1448 | tf_op jit(solution)/shard_map/ppermute | solution.py:22
  84.4 10.5 %collective-permute-start.13 = (f32[3,1,40,128]{3,2,0,1:T(8,128)S(1)}, f32[3,1,40,128]{3,2,0,1:T(8,128)S(1)}, u32[]{:S(2)}, u32[]{:S(2)}) collective-permute-start(f32[3,1,40,128]{3,2,0,1:T(8,128)S(1)} %broadcast_multiply_fusion.1), channel_id=1, source_target_pairs={{0,2},{2,4},{4,6},{6,8},{8,10},{10,12},{12,14},{14,16},{16,18},{18... | collective-permute-start | bytes 184328 | tf_op jit(solution)/shard_map/ppermute | solution.py:16
  88.3 6.5 %collective-permute-start.16 = (f32[3,1,40,1]{3,2,0,1:T(8,128)}, f32[3,1,40,1]{3,2,0,1:T(8,128)}, u32[]{:S(2)}, u32[]{:S(2)}) collective-permute-start(f32[3,1,40,1]{3,2,0,1:T(8,128)} %slice.784), channel_id=1, source_target_pairs={{1,0},{0,1},{3,2},{2,3},{5,4},{4,5},{7,6},{6,7},{9,8},{8,9},{11,10... | collective-permute-start | bytes 1448 | tf_op jit(solution)/shard_map/ppermute | solution.py:22
  90.0 9.2 %collective-permute-start.12 = (f32[3,1,40,128]{3,2,0,1:T(8,128)S(1)}, f32[3,1,40,128]{3,2,0,1:T(8,128)S(1)}, u32[]{:S(2)}, u32[]{:S(2)}) collective-permute-start(f32[3,1,40,128]{3,2,0,1:T(8,128)S(1)} %get-tuple-element.63), channel_id=1, source_target_pairs={{0,2},{2,4},{4,6},{6,8},{8,10},{10,12},{12,14},{14,16},{16,18},{18... | collective-permute-start | bytes 184328 | tf_op jit(solution)/shard_map/ppermute | solution.py:16
  94.3 4.9 %collective-permute-start.15 = (f32[3,1,40,1]{3,2,0,1:T(8,128)S(1)}, f32[3,1,40,1]{3,2,0,1:T(8,128)S(1)}, u32[]{:S(2)}, u32[]{:S(2)}) collective-permute-start(f32[3,1,40,1]{3,2,0,1:T(8,128)S(1)} %slice.781), channel_id=1, source_target_pairs={{1,0},{0,1},{3,2},{2,3},{5,4},{4,5},{7,6},{6,7},{9,8},{8,9},{11,10... | collective-permute-start | bytes 1448 | tf_op jit(solution)/shard_map/ppermute | solution.py:22
  100.3 6.1 %collective-permute-start.14 = (f32[3,1,40,128]{3,2,0,1:T(8,128)S(1)}, f32[3,1,40,128]{3,2,0,1:T(8,128)S(1)}, u32[]{:S(2)}, u32[]{:S(2)}) collective-permute-start(f32[3,1,40,128]{3,2,0,1:T(8,128)S(1)} %pad_maximum_fusion.8), channel_id=1, source_target_pairs={{2,0},{4,2},{6,4},{8,6},{10,8},{12,10},{14,12},{16,14},{18,16},{20... | collective-permute-start | bytes 184328 | tf_op jit(solution)/shard_map/ppermute | solution.py:16
  101.6 4.8 %collective-permute-start.17 = (f32[3,1,40,1]{3,2,0,1:T(8,128)S(1)}, f32[3,1,40,1]{3,2,0,1:T(8,128)S(1)}, u32[]{:S(2)}, u32[]{:S(2)}) collective-permute-start(f32[3,1,40,1]{3,2,0,1:T(8,128)S(1)} %bitcast.1517), channel_id=1, source_target_pairs={{1,0},{0,1},{3,2},{2,3},{5,4},{4,5},{7,6},{6,7},{9,8},{8,9},{11,10... | collective-permute-start | bytes 1448 | tf_op jit(solution)/shard_map/ppermute | solution.py:22
  107.2 11.8 %collective-permute-start.19 = (f32[3,1,40,128]{3,2,0,1:T(8,128)S(1)}, f32[3,1,40,128]{3,2,0,1:T(8,128)S(1)}, u32[]{:S(2)}, u32[]{:S(2)}) collective-permute-start(f32[3,1,40,128]{3,2,0,1:T(8,128)S(1)} %broadcast_multiply_fusion), channel_id=1, source_target_pairs={{0,2},{2,4},{4,6},{6,8},{8,10},{10,12},{12,14},{14,16},{16,18},{18... | collective-permute-start | bytes 184328 | tf_op jit(solution)/shard_map/ppermute | solution.py:16
  109.6 10.3 %collective-permute-start.18 = (f32[3,1,40,128]{3,2,0,1:T(8,128)S(1)}, f32[3,1,40,128]{3,2,0,1:T(8,128)S(1)}, u32[]{:S(2)}, u32[]{:S(2)}) collective-permute-start(f32[3,1,40,128]{3,2,0,1:T(8,128)S(1)} %get-tuple-element.60), channel_id=1, source_target_pairs={{0,2},{2,4},{4,6},{6,8},{8,10},{10,12},{12,14},{14,16},{16,18},{18... | collective-permute-start | bytes 184328 | tf_op jit(solution)/shard_map/ppermute | solution.py:16
  114.3 4.6 %collective-permute-start.22 = (f32[3,1,40,1]{3,2,0,1:T(8,128)S(1)}, f32[3,1,40,1]{3,2,0,1:T(8,128)S(1)}, u32[]{:S(2)}, u32[]{:S(2)}) collective-permute-start(f32[3,1,40,1]{3,2,0,1:T(8,128)S(1)} %slice.811), channel_id=1, source_target_pairs={{1,0},{0,1},{3,2},{2,3},{5,4},{4,5},{7,6},{6,7},{9,8},{8,9},{11,10... | collective-permute-start | bytes 1448 | tf_op jit(solution)/shard_map/ppermute | solution.py:22
  114.9 4.9 %collective-permute-start.21 = (f32[3,1,40,1]{3,2,0,1:T(8,128)S(1)}, f32[3,1,40,1]{3,2,0,1:T(8,128)S(1)}, u32[]{:S(2)}, u32[]{:S(2)}) collective-permute-start(f32[3,1,40,1]{3,2,0,1:T(8,128)S(1)} %slice.808), channel_id=1, source_target_pairs={{1,0},{0,1},{3,2},{2,3},{5,4},{4,5},{7,6},{6,7},{9,8},{8,9},{11,10... | collective-permute-start | bytes 1448 | tf_op jit(solution)/shard_map/ppermute | solution.py:22
  119.1 7.8 %copy-start.6 = (f32[3]{0:T(128)S(1)}, f32[3]{0:T(128)}, u32[]{:S(2)}) copy-start(f32[3]{0:T(128)} %get-tuple-element.154) | copy-start | bytes 40
  121.2 5.7 %collective-permute-start.23 = (f32[3,1,40,1]{3,2,0,1:T(8,128)S(1)}, f32[3,1,40,1]{3,2,0,1:T(8,128)S(1)}, u32[]{:S(2)}, u32[]{:S(2)}) collective-permute-start(f32[3,1,40,1]{3,2,0,1:T(8,128)S(1)} %bitcast.1513), channel_id=1, source_target_pairs={{1,0},{0,1},{3,2},{2,3},{5,4},{4,5},{7,6},{6,7},{9,8},{8,9},{11,10... | collective-permute-start | bytes 1448 | tf_op jit(solution)/shard_map/ppermute | solution.py:22
  122.2 4.8 %collective-permute-start.20 = (f32[3,1,40,128]{3,2,0,1:T(8,128)S(1)}, f32[3,1,40,128]{3,2,0,1:T(8,128)S(1)}, u32[]{:S(2)}, u32[]{:S(2)}) collective-permute-start(f32[3,1,40,128]{3,2,0,1:T(8,128)S(1)} %pad_maximum_fusion.11), channel_id=1, source_target_pairs={{2,0},{4,2},{6,4},{8,6},{10,8},{12,10},{14,12},{16,14},{18,16},{20... | collective-permute-start | bytes 184328 | tf_op jit(solution)/shard_map/ppermute | solution.py:16
  135.2 171.6 %copy-start.7 = (s32[2]{0:T(128)S(1)}, s32[2]{0:T(128)}, u32[]{:S(2)}) copy-start(s32[2]{0:T(128)} %iota_multiply_fusion) | copy-start | bytes 28
  (1 other events, 0.6 us)
Sparse Core Ops, SparseCore 0:
  141.7 126.5 all-reduce.15
where the time goes:
time: 345 us; the launch traced here: 343 us
  waiting for transfers between devices  143 us (41%)
  other arithmetic  84.9 us (25%)
  starting transfers between devices  44.5 us (13%)
  local copies, waits for them, and re-layouts  26.8 us (8%)
  between operations  26.1 us (8%)
  matrix products  18 us (5%)
    psum x1, waiting for transfers between devices, body(): lax.psum((mass_gram, projected), ('height', 'plan'))  126 us
    another operation x7, other arithmetic, body(): factor = jnp.linalg.cholesky(gram_total)  34.6 us
    ppermute x12, starting transfers between devices, passed_along(): return lax.ppermute(block, axis, route)  30.4 us
    another operation x4, other arithmetic, body(): coords_all = jax.scipy.linalg.cho_solve((factor, True), projected_total)  21.1 us
    ppermute x12, waiting for transfers between devices, from_behind(): return lax.ppermute(block, axis, route)  16 us
    ppermute x12, starting transfers between devices, from_behind(): return lax.ppermute(block, axis, route)  14 us
    dot_general x1, matrix products, body(): lax.dot_general(weighted, flat_modes, contract_last, preferred_element_ty...  8.41 us
    concatenate x1, local copies, waits for them, and re-layouts, body(): jnp.concatenate([snapshot_history, jnp.stack(new_snapshots)], axis=0)  8.1 us
  transfers between devices with their start and end apart: 25, of which 7 were waited for; matrix products, arithmetic and copies ran while one was open for 13% of the time, Pallas kernels for 0%

commit v1 on v0

v1 whole, which is shorter than its diff:
```python
import functools

import jax
import jax.numpy as jnp
from jax import lax
from jax.experimental import pallas as pl
from jax.experimental.pallas import tpu as pltpu
from jax.sharding import PartitionSpec as P

time_step = 0.3
mass_damping = 0.1
stiff_damping = 0.05
shear_stiff = 0.5
axial_components = (2, 1, 0)
HIGHEST = lax.Precision.HIGHEST
vmem_limit = 48 * 1024 * 1024


def mesh_id(linear, plan):
    return {"height": lax.div(linear, plan), "plan": lax.rem(linear, plan)}


def signal(semaphore, device):
    pl.semaphore_signal(semaphore, inc=1, device_id=device, device_id_type=pl.DeviceIdType.MESH)


def remote(source, target, send_sem, recv_sem, device):
    return pltpu.make_async_remote_copy(
        src_ref=source,
        dst_ref=target,
        send_sem=send_sem,
        recv_sem=recv_sem,
        device_id=device,
        device_id_type=pl.DeviceIdType.MESH,
    )


def greet_all(me, count, plan):
    barrier = pltpu.get_barrier_semaphore()

    def greet(offset, _):
        signal(barrier, mesh_id(lax.rem(me + offset, count), plan))
        return 0

    lax.fori_loop(1, count, greet, 0)
    return barrier


def wait_bytes(ref, semaphore):
    pltpu.make_async_copy(ref, ref, semaphore).wait()


def material_props(ids, table_ref):
    kinds = table_ref.shape[0]
    modulus = jnp.full(ids.shape, table_ref[0, 0], jnp.float32)
    yields = jnp.full(ids.shape, 0.4 * table_ref[0, 1], jnp.float32)
    slopes = jnp.full(ids.shape, 0.1 * table_ref[0, 2], jnp.float32)
    for kind in range(1, kinds):
        chosen = ids == kind
        modulus = jnp.where(chosen, table_ref[kind, 0], modulus)
        yields = jnp.where(chosen, 0.4 * table_ref[kind, 1], yields)
        slopes = jnp.where(chosen, 0.1 * table_ref[kind, 2], slopes)
    return modulus, yields, slopes, 1.0 / (modulus + slopes)


def fibre_step(stretch, plastic, harden, modulus, yields, slopes, inverse):
    trial = modulus * (stretch - plastic)
    excess = jnp.abs(trial) - (yields + slopes * harden)
    growth = jnp.maximum(excess, 0.0) * inverse
    signed = jnp.where(trial < 0.0, -growth, growth)
    return trial - modulus * signed, plastic + signed, harden + growth


def steps_kernel(
    heights, plan,
    disp_in, velo_in, mass_in, plastic_in, harden_in, ids_in, table_ref, accel_ref,
    disp_out, velo_out, plastic_out, harden_out, snaps_out,
    velos, props, top_plastic, top_harden, top_ids, top_props,
    near_disp, near_velo, edge_send, edge_recv,
    disp_send_sem, disp_recv_sem, velo_send_sem, velo_recv_sem, state_send_sem, state_recv_sem,
):
    h, p = lax.axis_index("height"), lax.axis_index("plan")
    fibres = plastic_in.shape[1]
    rows, columns = mass_in.shape
    steps = accel_ref.shape[0]
    has_below, has_above = h > 0, h < heights - 1
    below = {"height": h - 1, "plan": p}
    above = {"height": h + 1, "plan": p}
    left = {"height": h, "plan": lax.rem(p + plan - 1, plan)}
    right = {"height": h, "plan": lax.rem(p + 1, plan)}
    lane = lax.broadcasted_iota(jnp.int32, (rows, columns), 1)
    row = lax.broadcasted_iota(jnp.int32, (rows, columns), 0)
    last = columns - 1

    barrier = pltpu.get_barrier_semaphore()

    @pl.when(has_below)
    def _():
        signal(barrier, below)

    @pl.when(has_above)
    def _():
        signal(barrier, above)

    signal(barrier, left)
    signal(barrier, right)

    velos[0] = velo_in[...]
    packed = [jnp.zeros((rows, columns), jnp.float32) for _ in range(3)]
    for f in range(fibres):
        for part, value in enumerate(
            (plastic_in[2, f], harden_in[2, f], ids_in[2, f].astype(jnp.float32))
        ):
            packed[part] = jnp.where(lane == f, value[:, 0:1], packed[part])
    for part in range(3):
        edge_send[part] = packed[part]

    greetings = 2 + has_below.astype(jnp.int32) + has_above.astype(jnp.int32)
    pl.semaphore_wait(barrier, greetings)

    def disp_copy(side, device):
        return remote(
            disp_in, near_disp.at[side], disp_send_sem.at[side], disp_recv_sem.at[side], device
        )

    def velo_copy(side, step, device):
        return remote(
            velos.at[step], near_velo.at[step, side],
            velo_send_sem.at[step, side], velo_recv_sem.at[step, side], device,
        )

    def state_copies():
        return [
            remote(plastic_in.at[0], top_plastic, state_send_sem.at[0], state_recv_sem.at[0], below),
            remote(harden_in.at[0], top_harden, state_send_sem.at[1], state_recv_sem.at[1], below),
            remote(ids_in.at[0], top_ids, state_send_sem.at[2], state_recv_sem.at[2], below),
        ]

    edge_copy = remote(edge_send, edge_recv, state_send_sem.at[3], state_recv_sem.at[3], left)

    def exchange(step, first):
        copies = [lambda s, d: velo_copy(s, step, d)]
        if first:
            copies.append(disp_copy)

        @pl.when(has_above)
        def _():
            for make in copies:
                make(0, above).start()

        @pl.when(has_below)
        def _():
            for make in copies:
                make(1, below).start()

        for make in copies:
            make(2, right).start()
            make(3, left).start()

    def finish(step, first):
        copies = [lambda s, d: velo_copy(s, step, d)]
        if first:
            copies.append(disp_copy)

        @pl.when(has_below)
        def _():
            for make in copies:
                make(0, below).wait_recv()
                make(1, below).wait_send()

        @pl.when(has_above)
        def _():
            for make in copies:
                make(1, above).wait_recv()
                make(0, above).wait_send()

        for make in copies:
            for side, device in ((2, right), (3, left)):
                make(side, device).wait()

    exchange(0, True)
    edge_copy.start()

    @pl.when(has_below)
    def _():
        for copy in state_copies():
            copy.start()

    @pl.when(jnp.logical_not(has_below))
    def _():
        near_disp[0] = jnp.zeros(near_disp.shape[1:], jnp.float32)
        for step in range(steps):
            near_velo[step, 0] = jnp.zeros(near_velo.shape[2:], jnp.float32)

    @pl.when(jnp.logical_not(has_above))
    def _():
        near_disp[1] = jnp.zeros(near_disp.shape[1:], jnp.float32)
        for step in range(steps):
            near_velo[step, 1] = jnp.zeros(near_velo.shape[2:], jnp.float32)
        top_plastic[...] = jnp.zeros(top_plastic.shape, jnp.float32)
        top_harden[...] = jnp.zeros(top_harden.shape, jnp.float32)
        top_ids[...] = jnp.zeros(top_ids.shape, jnp.int32)

    zero = jnp.zeros((rows, columns), jnp.float32)

    def own_props(f, sums):
        new_sums = []
        for b in range(3):
            found = material_props(ids_in[b, f], table_ref)
            for part in range(4):
                props[part, b, f] = found[part]
            new_sums.append(sums[b] + found[0])
        return tuple(new_sums)

    sums = lax.fori_loop(0, fibres, own_props, (zero, zero, zero))
    tangents = [total * (1.0 / fibres) for total in sums]

    finish(0, True)
    edge_copy.wait()

    @pl.when(has_below)
    def _():
        for copy in state_copies():
            copy.wait_send()

    @pl.when(has_above)
    def _():
        for copy in state_copies():
            copy.wait_recv()

    def above_props(f, total):
        found = material_props(top_ids[f], table_ref)
        for part in range(4):
            top_props[part, f] = found[part]
        return total + found[0]

    top_tangent = lax.fori_loop(0, fibres, above_props, zero) * (1.0 / fibres)

    in_edge = lane < fibres
    edge_plastic, edge_harden = edge_recv[0], edge_recv[1]
    edge_found = material_props(edge_recv[2].astype(jnp.int32), table_ref)

    def edge_mean(value):
        return jnp.sum(jnp.where(in_edge, value, 0.0), axis=1, keepdims=True) * (1.0 / fibres)

    edge_tangent = edge_mean(edge_found[0])

    disp = [disp_in[c] for c in range(3)]
    velo = [velo_in[c] for c in range(3)]
    mass_inverse = 1.0 / mass_in[...]

    def rows_before(x):
        return jnp.where(row == 0, 0.0, pltpu.roll(x, 1, 0))

    def rows_after(x):
        return jnp.where(row == rows - 1, 0.0, pltpu.roll(x, rows - 1, 0))

    def rim_before(x, left_block):
        return pltpu.roll(jnp.where(lane == last, left_block, x), 1, 1)

    def shear(stretch, rate):
        return shear_stiff * (stretch + stiff_damping * rate)

    for step in range(steps):
        if step > 0:
            finish(step, False)
            for side in range(4):
                for c in range(3):
                    near_disp[side, c] = near_disp[side, c] + time_step * near_velo[step, side, c]
        source_plastic, source_harden = (
            (plastic_in, harden_in) if step == 0 else (plastic_out, harden_out)
        )
        stretch = [
            [disp[c] - near_disp[0, c] for c in range(3)],
            [disp[c] - rows_before(disp[c]) for c in range(3)],
            [disp[c] - rim_before(disp[c], near_disp[2, c]) for c in range(3)],
        ]
        rate = [
            [velo[c] - near_velo[step, 0, c] for c in range(3)],
            [velo[c] - rows_before(velo[c]) for c in range(3)],
            [velo[c] - rim_before(velo[c], near_velo[step, 2, c]) for c in range(3)],
        ]
        top_stretch = [near_disp[1, c] - disp[c] for c in range(3)]
        top_rate = [near_velo[step, 1, c] - velo[c] for c in range(3)]
        rim_stretch = [near_disp[3, c][:, 0:1] - disp[c][:, last:] for c in range(3)]
        rim_rate = [near_velo[step, 3, c][:, 0:1] - velo[c][:, last:] for c in range(3)]

        def fibre(f, totals):
            new_totals = []
            for b in range(3):
                stress, plastic, harden = fibre_step(
                    stretch[b][axial_components[b]], source_plastic[b, f], source_harden[b, f],
                    props[0, b, f], props[1, b, f], props[2, b, f], props[3, b, f],
                )
                plastic_out[b, f] = plastic
                harden_out[b, f] = harden
                new_totals.append(totals[b] + stress)
            stress, plastic, harden = fibre_step(
                top_stretch[axial_components[0]], top_plastic[f], top_harden[f],
                top_props[0, f], top_props[1, f], top_props[2, f], top_props[3, f],
            )
            top_plastic[f] = plastic
            top_harden[f] = harden
            new_totals.append(totals[3] + stress)
            return tuple(new_totals)

        totals = lax.fori_loop(0, fibres, fibre, (zero, zero, zero, zero))
        edge_stress, edge_plastic, edge_harden = fibre_step(
            rim_stretch[axial_components[2]], edge_plastic, edge_harden, *edge_found
        )
        edge_axial = edge_mean(edge_stress)

        new_velo = []
        for c in range(3):
            force = []
            for b in range(3):
                if c == axial_components[b]:
                    force.append(
                        totals[b] * (1.0 / fibres) + stiff_damping * tangents[b] * rate[b][c]
                    )
                else:
                    force.append(shear(stretch[b][c], rate[b][c]))
            if c == axial_components[0]:
                top = totals[3] * (1.0 / fibres) + stiff_damping * top_tangent * top_rate[c]
            else:
                top = shear(top_stretch[c], top_rate[c])
            if c == axial_components[2]:
                rim = edge_axial + stiff_damping * edge_tangent * rim_rate[c]
            else:
                rim = shear(rim_stretch[c], rim_rate[c])
            top = jnp.where(has_above, top, 0.0)
            after_rim = jnp.where(lane == last, rim, pltpu.roll(force[2], last, 1))
            resisting = (
                force[0] - top + (force[1] - rows_after(force[1])) + (force[2] - after_rim)
            )
            acceleration = -accel_ref[step, c] - resisting * mass_inverse
            new_velo.append(
                ((1.0 - 0.5 * mass_damping * time_step) * velo[c] + time_step * acceleration)
                * (1.0 / (1.0 + 0.5 * mass_damping * time_step))
            )
        velo = new_velo
        if step + 1 < steps:
            for c in range(3):
                velos[step + 1, c] = velo[c]
            exchange(step + 1, False)
        for c in range(3):
            disp[c] = disp[c] + time_step * velo[c]
            snaps_out[step, c] = disp[c].astype(jnp.bfloat16)
    for c in range(3):
        disp_out[c] = disp[c]
        velo_out[c] = velo[c]


def run_steps(disp, velo, mass, plastic, harden, ids, table, accel):
    heights, plan = lax.axis_size("height"), lax.axis_size("plan")
    steps = accel.shape[0]
    vmem = pl.BlockSpec(memory_space=pltpu.VMEM)
    smem = pl.BlockSpec(memory_space=pltpu.SMEM)
    f32 = jnp.float32
    fibres = plastic.shape[1]
    plane = mass.shape
    return pl.pallas_call(
        functools.partial(steps_kernel, heights, plan),
        out_shape=(
            jax.ShapeDtypeStruct(disp.shape, f32),
            jax.ShapeDtypeStruct(velo.shape, f32),
            jax.ShapeDtypeStruct(plastic.shape, f32),
            jax.ShapeDtypeStruct(harden.shape, f32),
            jax.ShapeDtypeStruct((steps,) + disp.shape, jnp.bfloat16),
        ),
        in_specs=[vmem] * 6 + [smem] * 2,
        out_specs=(vmem,) * 5,
        scratch_shapes=[
            pltpu.VMEM((steps,) + velo.shape, f32),
            pltpu.VMEM((4,) + plastic.shape, f32),
            pltpu.VMEM((fibres,) + plane, f32),
            pltpu.VMEM((fibres,) + plane, f32),
            pltpu.VMEM((fibres,) + plane, jnp.int32),
            pltpu.VMEM((4, fibres) + plane, f32),
            pltpu.VMEM((4,) + disp.shape, f32),
            pltpu.VMEM((steps, 4) + velo.shape, f32),
            pltpu.VMEM((3,) + plane, f32),
            pltpu.VMEM((3,) + plane, f32),
            pltpu.SemaphoreType.DMA((4,)),
            pltpu.SemaphoreType.DMA((4,)),
            pltpu.SemaphoreType.DMA((steps, 4)),
            pltpu.SemaphoreType.DMA((steps, 4)),
            pltpu.SemaphoreType.DMA((4,)),
            pltpu.SemaphoreType.DMA((4,)),
        ],
        compiler_params=pltpu.CompilerParams(
            collective_id=0, has_side_effects=True, vmem_limit_bytes=vmem_limit
        ),
        name="time_steps",
    )(disp, velo, mass, plastic, harden, ids, table, accel)


def gram_kernel(
    count, plan, part_ref, out_ref, landed, total, send_sem, recv_sem, give_sem, take_sem
):
    me = lax.axis_index("height") * plan + lax.axis_index("plan")
    barrier = greet_all(me, count, plan)
    pl.semaphore_wait(barrier, count - 1)

    def send(offset, _):
        target = lax.rem(me + offset, count)
        remote(
            part_ref.at[target], landed.at[offset - 1], send_sem, recv_sem, mesh_id(target, plan)
        ).start()
        return 0

    lax.fori_loop(1, count, send, 0)
    wait_bytes(landed, recv_sem)
    total[...] = part_ref[me] + jnp.sum(landed[...], axis=0)

    def give(offset, _):
        target = lax.rem(me + offset, count)
        remote(total, out_ref.at[me], give_sem, take_sem, mesh_id(target, plan)).start()
        return 0

    lax.fori_loop(1, count, give, 0)
    out_ref[me] = total[...]
    wait_bytes(landed, take_sem)
    wait_bytes(landed, send_sem)
    wait_bytes(landed, give_sem)


def gram_total(part):
    plan = lax.axis_size("plan")
    count = lax.axis_size(("height", "plan"))
    modes = part.shape[0]
    rows = modes // count
    vmem = pl.BlockSpec(memory_space=pltpu.VMEM)
    out = pl.pallas_call(
        functools.partial(gram_kernel, count, plan),
        out_shape=jax.ShapeDtypeStruct((count, rows, modes), jnp.float32),
        in_specs=[vmem],
        out_specs=vmem,
        scratch_shapes=[
            pltpu.VMEM((count - 1, rows, modes), jnp.float32),
            pltpu.VMEM((rows, modes), jnp.float32),
        ] + [pltpu.SemaphoreType.DMA] * 4,
        compiler_params=pltpu.CompilerParams(
            collective_id=1, has_side_effects=True, vmem_limit_bytes=vmem_limit
        ),
        name="gram_sum",
    )(part.reshape(count, rows, modes))
    return out.reshape(modes, modes)


def coords_kernel(count, plan, part_ref, out_ref, landed, send_sem, recv_sem):
    me = lax.axis_index("height") * plan + lax.axis_index("plan")
    barrier = greet_all(me, count, plan)
    pl.semaphore_wait(barrier, count - 1)

    def send(offset, _):
        target = lax.rem(me + offset, count)
        remote(
            part_ref.at[target], landed.at[offset - 1], send_sem, recv_sem, mesh_id(target, plan)
        ).start()
        return 0

    lax.fori_loop(1, count, send, 0)
    wait_bytes(landed, recv_sem)
    out_ref[...] = part_ref[me] + jnp.sum(landed[...], axis=0)
    wait_bytes(landed, send_sem)


def coords_total(part):
    plan = lax.axis_size("plan")
    count = lax.axis_size(("height", "plan"))
    modes, snaps = part.shape
    rows = modes // count
    vmem = pl.BlockSpec(memory_space=pltpu.VMEM)
    return pl.pallas_call(
        functools.partial(coords_kernel, count, plan),
        out_shape=jax.ShapeDtypeStruct((rows, snaps), jnp.float32),
        in_specs=[vmem],
        out_specs=vmem,
        scratch_shapes=[pltpu.VMEM((count - 1, rows, snaps), jnp.float32)]
        + [pltpu.SemaphoreType.DMA] * 2,
        compiler_params=pltpu.CompilerParams(
            collective_id=2, has_side_effects=True, vmem_limit_bytes=vmem_limit
        ),
        name="coords_sum",
    )(part.reshape(count, rows, snaps))


def solve_kernel(gram_ref, projected_ref, out_ref):
    modes = gram_ref.shape[0]
    row = lax.broadcasted_iota(jnp.int32, (modes, modes), 0)
    column = lax.broadcasted_iota(jnp.int32, (modes, modes), 1)
    lower = jnp.where(row >= column, gram_ref[...], 0.0)
    gram = lower + jnp.where(row == column, 0.0, lower).T
    identity = jnp.where(row == column, 1.0, 0.0)
    size = jnp.max(jnp.sum(jnp.abs(gram), axis=1))
    guess = identity * (1.0 / size)

    def multiply(a, b):
        return jnp.dot(a, b, precision=HIGHEST, preferred_element_type=jnp.float32)

    def unfinished(state):
        turns, error, _ = state
        return jnp.logical_and(turns < 60, error > 1e-3)

    def improve(state):
        turns, _, inverse = state
        residual = identity - multiply(gram, inverse)
        error = jnp.max(jnp.sum(jnp.abs(residual), axis=0))
        return turns + 1, error, inverse + multiply(inverse, residual)

    _, _, inverse = lax.while_loop(unfinished, improve, (0, jnp.float32(2.0), guess))
    out_ref[...] = multiply(inverse, projected_ref[...])


def solve(gram, projected):
    vmem = pl.BlockSpec(memory_space=pltpu.VMEM)
    return pl.pallas_call(
        solve_kernel,
        out_shape=jax.ShapeDtypeStruct(projected.shape, jnp.float32),
        in_specs=[vmem, vmem],
        out_specs=vmem,
        compiler_params=pltpu.CompilerParams(vmem_limit_bytes=vmem_limit),
        name="solve",
    )(gram, projected)


def body(
    displacement,
    velocity,
    lumped_mass,
    plastic_strain,
    hardening_strain,
    material_ids,
    material_table,
    ground_accel,
    snapshot_history,
    mode_shapes,
):
    mode_count = mode_shapes.shape[0]
    flat_modes = mode_shapes.reshape(mode_count, -1)
    weighted = (
        (mode_shapes.astype(jnp.float32) * lumped_mass[None, None])
        .astype(jnp.bfloat16)
        .reshape(mode_count, -1)
    )
    contract_last = (((1,), (1,)), ((), ()))
    mass_gram = lax.dot_general(
        weighted, flat_modes, contract_last, preferred_element_type=jnp.float32
    )
    flat_history = snapshot_history.reshape(snapshot_history.shape[0], -1)
    projected_history = lax.dot_general(
        weighted, flat_history, contract_last, preferred_element_type=jnp.float32
    )
    gram = gram_total(mass_gram)
    disp_end, velo_end, plastic_end, harden_end, new_snaps = run_steps(
        displacement[:, 0], velocity[:, 0], lumped_mass[0], plastic_strain[:, :, 0],
        hardening_strain[:, :, 0], material_ids[:, :, 0], material_table, ground_accel,
    )
    projected_new = lax.dot_general(
        weighted, new_snaps.reshape(new_snaps.shape[0], -1), contract_last,
        preferred_element_type=jnp.float32,
    )
    projected = jnp.concatenate([projected_history, projected_new], axis=1)
    modal_coords = coords_total(solve(gram, projected))
    return (
        disp_end[:, None], velo_end[:, None], plastic_end[:, :, None], harden_end[:, :, None],
        modal_coords,
    )


def solution(mesh):
    return jax.shard_map(
        body,
        mesh=mesh,
        in_specs=(
            P(None, "height", None, "plan"),
            P(None, "height", None, "plan"),
            P("height", None, "plan"),
            P(None, None, "height", None, "plan"),
            P(None, None, "height", None, "plan"),
            P(None, None, "height", None, "plan"),
            P(),
            P(),
            P(None, None, "height", None, "plan"),
            P(None, None, "height", None, "plan"),
        ),
        out_specs=(
            P(None, "height", None, "plan"),
            P(None, "height", None, "plan"),
            P(None, None, "height", None, "plan"),
            P(None, None, "height", None, "plan"),
            P(("height", "plan"), None),
        ),
        check_vma=False,
    )
```

time: 345 us -> 145 us (0.42)
  waiting for transfers between devices: 143 us -> 0 us
  Pallas kernels: 0 us -> 73.9 us
  other arithmetic: 84.9 us -> 15.9 us
  starting transfers between devices: 44.5 us -> 0 us
  between operations: 26.1 us -> 0.72 us
  local copies, waits for them, and re-layouts: 26.8 us -> 34.7 us
    psum x1 -> x0, waiting for transfers between devices: 126 us -> none  [body(): lax.psum((mass_gram, projected), ('height', 'plan'))]
    pallas_call x0 -> x4, Pallas kernels: none -> 73.9 us  [the longest x1 29.8 us: run_steps(): pl.pallas_call(functools.partial(steps_kernel, heights, plan), out_shape=...]
    another operation x30 -> x1, other arithmetic: 66.3 us -> 7.9 us  [the longest x7 34.6 us: body(): factor = jnp.linalg.cholesky(gram_total)]
    ppermute x24 -> x0, starting transfers between devices: 44.4 us -> none  [the longest x12 30.4 us: passed_along(): return lax.ppermute(block, axis, route)]
    ppermute x24 -> x0, waiting for transfers between devices: 16.7 us -> none  [the longest x12 16 us: from_behind(): return lax.ppermute(block, axis, route)]
    dot_general x0 -> x1, local copies, waits for them, and re-layouts: none -> 11.7 us  [body(): lax.dot_general(weighted, flat_modes, contract_last, preferred_element_ty...]
    reshape x0 -> x1, local copies, waits for them, and re-layouts: none -> 11.2 us  [body(): flat_modes = mode_shapes.reshape(mode_count, -1)]
    add x21 -> x0, other arithmetic: 10.1 us -> none  [the longest x1 6.53 us: fibre_props(): modulus = modulus + selected * material_table[material_index, 0]]
  transfers between devices with their start and end apart: 25 -> 0, of which waited for: 7 -> 0; matrix products, arithmetic and copies ran while one was open for 13% -> 0% of each run, Pallas kernels for 0% -> 0%
where the time goes in v1:
time: 145 us; the launch traced here: 144 us
  Pallas kernels  73.9 us (51%)
  local copies, waits for them, and re-layouts  34.7 us (24%)
  matrix products  18.5 us (13%)
  other arithmetic  15.9 us (11%)
    pallas_call x1, Pallas kernels, run_steps(): pl.pallas_call(functools.partial(steps_kernel, heights, plan), out_shape=...  29.8 us
    pallas_call x1, Pallas kernels, gram_total(): pl.pallas_call(functools.partial(gram_kernel, count, plan), out_shape=jax...  18.3 us
    pallas_call x1, Pallas kernels, solve(): pl.pallas_call(solve_kernel, out_shape=jax.ShapeDtypeStruct(projected.sha...  16.5 us
    unnamed x24, local copies, waits for them, and re-layouts  11.8 us
    dot_general x1, local copies, waits for them, and re-layouts, body(): lax.dot_general(weighted, flat_modes, contract_last, preferred_element_ty...  11.7 us
    reshape x1, local copies, waits for them, and re-layouts, body(): flat_modes = mode_shapes.reshape(mode_count, -1)  11.2 us
    pallas_call x1, Pallas kernels, coords_total(): pl.pallas_call(functools.partial(coords_kernel, count, plan), out_shape=j...  9.27 us
    convert_element_type x1, other arithmetic, body(): weighted = (mode_shapes.astype(jnp.float32) * lumped_mass[None, None]).as...  7.9 us

profile of v1, /device:TPU:0, one launch (start us, length us, event | category | flops | bytes accessed | tf_op | source)
XLA Modules:
  0.0 143.7 jit_solution(17911751849665560213)
XLA Ops:
  0.6 0.0 copy-start
  0.6 1.5 %copy-done = bf16[60,3,1,40,128]{4,3,2,1,0:T(8,128)(2,1)S(1)} copy-done((bf16[60,3,1,40,128]{4,3,2,1,0:T(8,128)(2,1)S(1)}, bf16[60,3,1,40,128]{4,3,2,1,0:T(8,128)(2,1)}, u32[]{:S(2)}) %copy-start) | copy-done | bytes 1843224
  2.1 0.8 copy.15.table_ref
  2.9 0.0 copy-start.1
  2.9 1.0 copy-done.1
  3.9 0.0 copy-start.2
  3.9 1.0 copy-done.2
  5.0 0.0 copy-start.3
  5.0 1.0 copy-done.3
  6.0 0.7 copy-done.4
  6.7 0.8 copy-done.6
  7.5 0.8 copy-done.7
  8.4 0.7 copy-done.8
  9.1 29.8 %time_steps.1 = (f32[3,40,128]{2,1,0:T(8,128)S(1)}, f32[3,40,128]{2,1,0:T(8,128)S(1)}, f32[3,8,40,128]{3,2,1,0:T(8,128)S(1)}, f32[3,8,40,128]{3,2,1,0:T(8,128)S(1)}, bf16[4,3,40,128]{3,2,1,0:T(8,128)(2,1)S(1)}) custom-call(f32[3,40,128]{2,1,0:T(8,128)S(1)} %bitcast.52, f32[3,40,128]{2,1,0:T(8,128)S(1)} %bitcast.53, f32[40,128]{1,0:T(8,128)S(1)} %bitcast.50, ...), custom_call_target="tpu_custom_call" | custom-call | tf_op jit(solution)/shard_map/time_steps/pallas_call | solution.py:362
  38.8 7.9 %multiply_convert_fusion = bf16[256,3,1,40,128]{4,3,2,1,0:T(8,128)(2,1)} fusion(bf16[256,3,1,40,128]{4,3,2,1,0:T(8,128)(2,1)} %param.19, f32[40,128]{1,0:T(8,128)} %bitcast.49), kind=kLoop, calls=%fused_computation | loop fusion | flops 11796480 | bytes 15749120 | tf_op jit(solution)/shard_map/convert_element_type | solution.py:544
  46.7 5.4 %fusion = f32[256,4]{1,0:T(8,128)S(1)} fusion(bf16[32,8,120,128]{3,2,1,0:T(8,128)(2,1)} %bitcast.57, bf16[1,4,120,128]{3,2,1,0:T(8,128)(2,1)S(1)} %bitcast.56), kind=kOutput, calls=%fused_computation.1 | convolution fusion | flops 31457280 | bytes 7991296 | tf_op jit(solution)/shard_map/dot_general | solution.py:560
  52.1 0.0 copy-start.5
  52.1 11.7 %dot_general.11 = bf16[32,8,15360]{2,1,0:T(8,128)(2,1)} reshape(bf16[256,3,1,40,128]{4,3,2,1,0:T(8,128)(2,1)} %multiply_convert_fusion) | data formatting | bytes 15728640 | tf_op jit(solution)/shard_map/dot_general | solution.py:548
  63.9 0.0 copy-done.5
  63.9 7.9 %fusion.16 = bf16[256,3,40,128]{3,2,1,0:T(8,128)(2,1)} fusion(f32[40,128]{1,0:T(8,128)S(1)} %bitcast.51, bf16[256,3,1,40,128]{4,3,2,1,0:T(8,128)(2,1)} %param.19), kind=kLoop, calls=%fused_computation.12 | loop fusion | flops 11796480 | bytes 15749120 | tf_op jit(solution)/shard_map/reshape.5
  71.8 5.4 %fusion.6 = f32[256,60]{1,0:T(8,128)S(1)} fusion(bf16[60,3,40,128]{3,2,1,0:T(8,128)(2,1)S(1)} %bitcast.41, bf16[256,3,40,128]{3,2,1,0:T(8,128)(2,1)} %fusion.16), kind=kOutput, calls=%fused_computation.7 | convolution fusion | flops 471859200 | bytes 9768960 | tf_op jit(solution)/shard_map/dot_general | solution.py:552
  77.2 0.1 pad_maximum_fusion.projected_ref
  77.3 11.2 %reshape.45 = bf16[256,15360,1]{1,0,2:T(8,128)(2,1)} reshape(bf16[256,3,1,40,128]{4,3,2,1,0:T(8,128)(2,1)} %param.19) | data formatting | bytes 15728640 | tf_op jit(solution)/shard_map/reshape | solution.py:541
  88.4 7.7 %fusion.13.part_ref = f32[32,8,256]{2,1,0:T(8,128)S(1)} fusion(bf16[32,8,15360]{2,1,0:T(8,128)(2,1)} %dot_general.11, bf16[256,15360,1]{1,0,2:T(8,128)(2,1)} %reshape.45), kind=kOutput, calls=%fused_computation.11 | convolution fusion | flops 2013265920 | bytes 15990784 | tf_op jit(solution)/shard_map/dot_general | solution.py:548
  96.1 18.3 %gram_sum.1 = f32[32,8,256]{2,1,0:T(8,128)S(1)} custom-call(f32[32,8,256]{2,1,0:T(8,128)S(1)} %fusion.13.part_ref), custom_call_target="tpu_custom_call" | custom-call | tf_op jit(solution)/shard_map/gram_sum/pallas_call | solution.py:434
  114.5 16.5 %solve.1 = f32[256,64]{1,0:T(8,128)S(1)} custom-call(f32[256,256]{1,0:T(8,128)S(1)} %bitcast.42, f32[256,64]{1,0:T(8,128)S(1)} %pad_maximum_fusion.projected_ref), custom_call_target="tpu_custom_call" | custom-call | tf_op jit(solution)/shard_map/solve/pallas_call | solution.py:518
  131.0 9.3 %coords_sum.1 = f32[8,64]{1,0:T(8,128)S(1)} custom-call(f32[32,8,64]{2,1,0:T(8,128)S(1)} %bitcast.43), custom_call_target="tpu_custom_call" | custom-call | tf_op jit(solution)/shard_map/coords_sum/pallas_call | solution.py:475
  140.3 0.6 copy.50
  140.9 0.6 copy.51
  141.5 0.8 copy.52
  142.3 0.8 copy.53
  143.1 0.6 copy.54
  (4 shorter events, 0.0 us)
Async XLA Ops:
  0.6 1.5 %copy-start = (bf16[60,3,1,40,128]{4,3,2,1,0:T(8,128)(2,1)S(1)}, bf16[60,3,1,40,128]{4,3,2,1,0:T(8,128)(2,1)}, u32[]{:S(2)}) copy-start(bf16[60,3,1,40,128]{4,3,2,1,0:T(8,128)(2,1)} %param.18) | copy-start | bytes 5529604
  2.9 1.0 copy-start.1
  3.9 1.0 copy-start.2
  5.0 1.0 copy-start.3
  6.0 0.7 copy-start.4
  6.7 0.8 copy-start.6
  7.5 0.8 copy-start.7
  8.4 0.7 copy-start.8
  52.1 11.7 %copy-start.5 = (f32[1,40,128]{2,1,0:T(8,128)S(1)}, f32[1,40,128]{2,1,0:T(8,128)}, u32[]{:S(2)}) copy-start(f32[1,40,128]{2,1,0:T(8,128)} %param.12) | copy-start | bytes 61444

commit v2 on v1

--- a/solution.py
+++ b/solution.py
@@ -1,4 +1,5 @@
 import functools
+import math
 
 import jax
 import jax.numpy as jnp
@@ -525,6 +526,93 @@
     )(gram, projected)
 
 
+def products_kernel(
+    modes_ref, mass_ref, history_ref, recent_ref, gram_ref, projected_ref, modes_wide, snaps_wide
+):
+    modes, rows, columns = modes_ref.shape
+    earlier, recent = history_ref.shape[0], recent_ref.shape[0]
+    snaps = earlier + recent
+    chunk = math.gcd(modes, 16)
+    group = math.gcd(rows, 8)
+
+    def widen(i, _):
+        block = modes_ref[pl.ds(i * chunk, chunk)].astype(jnp.float32)
+        modes_wide[pl.ds(pl.multiple_of(i * chunk * rows, 8), chunk * rows), :] = block.reshape(
+            chunk * rows, columns
+        )
+        return 0
+
+    lax.fori_loop(0, modes // chunk, widen, 0)
+
+    def widen_history(i, _):
+        snaps_wide[pl.ds(pl.multiple_of(i * rows, 8), rows), :] = history_ref[i].astype(jnp.float32)
+        return 0
+
+    lax.fori_loop(0, earlier, widen_history, 0)
+    for i in range(recent):
+        snaps_wide[pl.ds((earlier + i) * rows, rows), :] = recent_ref[i].astype(jnp.float32)
+
+    @pl.when(pl.program_id(0) == 0)
+    def _():
+        gram_ref[...] = jnp.zeros(gram_ref.shape, jnp.float32)
+        projected_ref[...] = jnp.zeros(projected_ref.shape, jnp.float32)
+
+    contract_last = (((1,), (1,)), ((), ()))
+
+    def add(i, _):
+        weighted, plain, shots = [], [], []
+        masses = mass_ref[pl.ds(pl.multiple_of(i * group, group), group), :]
+        for j in range(group):
+            row = i * group + j
+            shape = modes_wide[pl.ds(row, modes, stride=rows), :]
+            weighted.append((shape * masses[j : j + 1, :]).astype(jnp.bfloat16))
+            plain.append(shape.astype(jnp.bfloat16))
+            shots.append(snaps_wide[pl.ds(row, snaps, stride=rows), :].astype(jnp.bfloat16))
+        left = jnp.concatenate(weighted, axis=1)
+        gram_ref[...] += lax.dot_general(
+            left, jnp.concatenate(plain, axis=1), contract_last,
+            preferred_element_type=jnp.float32,
+        )
+        projected_ref[...] += lax.dot_general(
+            left, jnp.concatenate(shots, axis=1), contract_last,
+            preferred_element_type=jnp.float32,
+        )
+        return 0
+
+    lax.fori_loop(0, rows // group, add, 0)
+
+
+def products(mode_shapes, mass, history, recent):
+    modes, parts, rows, columns = mode_shapes.shape
+    earlier, later = history.shape[0], recent.shape[0]
+    snaps = earlier + later
+    f32 = jnp.float32
+    return pl.pallas_call(
+        products_kernel,
+        grid=(parts,),
+        out_shape=(
+            jax.ShapeDtypeStruct((modes, modes), f32),
+            jax.ShapeDtypeStruct((modes, snaps), f32),
+        ),
+        in_specs=[
+            pl.BlockSpec((modes, None, rows, columns), lambda c: (0, c, 0, 0)),
+            pl.BlockSpec((rows, columns), lambda c: (0, 0)),
+            pl.BlockSpec((earlier, None, rows, columns), lambda c: (0, c, 0, 0)),
+            pl.BlockSpec((later, None, rows, columns), lambda c: (0, c, 0, 0)),
+        ],
+        out_specs=(
+            pl.BlockSpec((modes, modes), lambda c: (0, 0)),
+            pl.BlockSpec((modes, snaps), lambda c: (0, 0)),
+        ),
+        scratch_shapes=[
+            pltpu.VMEM((modes * rows, columns), f32),
+            pltpu.VMEM((snaps * rows, columns), f32),
+        ],
+        compiler_params=pltpu.CompilerParams(vmem_limit_bytes=vmem_limit),
+        name="products",
+    )(mode_shapes, mass, history, recent)
+
+
 def body(
     displacement,
     velocity,
@@ -537,31 +625,14 @@
     snapshot_history,
     mode_shapes,
 ):
-    mode_count = mode_shapes.shape[0]
-    flat_modes = mode_shapes.reshape(mode_count, -1)
-    weighted = (
-        (mode_shapes.astype(jnp.float32) * lumped_mass[None, None])
-        .astype(jnp.bfloat16)
-        .reshape(mode_count, -1)
-    )
-    contract_last = (((1,), (1,)), ((), ()))
-    mass_gram = lax.dot_general(
-        weighted, flat_modes, contract_last, preferred_element_type=jnp.float32
-    )
-    flat_history = snapshot_history.reshape(snapshot_history.shape[0], -1)
-    projected_history = lax.dot_general(
-        weighted, flat_history, contract_last, preferred_element_type=jnp.float32
-    )
-    gram = gram_total(mass_gram)
     disp_end, velo_end, plastic_end, harden_end, new_snaps = run_steps(
         displacement[:, 0], velocity[:, 0], lumped_mass[0], plastic_strain[:, :, 0],
         hardening_strain[:, :, 0], material_ids[:, :, 0], material_table, ground_accel,
     )
-    projected_new = lax.dot_general(
-        weighted, new_snaps.reshape(new_snaps.shape[0], -1), contract_last,
-        preferred_element_type=jnp.float32,
+    mass_gram, projected = products(
+        mode_shapes[:, :, 0], lumped_mass[0], snapshot_history[:, :, 0], new_snaps
     )
-    projected = jnp.concatenate([projected_history, projected_new], axis=1)
+    gram = gram_total(mass_gram)
     modal_coords = coords_total(solve(gram, projected))
     return (
         disp_end[:, None], velo_end[:, None], plastic_end[:, :, None], harden_end[:, :, None],

time: 145 us -> 98.2 us (0.68)
  local copies, waits for them, and re-layouts: 34.7 us -> 11.8 us
  matrix products: 18.5 us -> 0 us
  other arithmetic: 15.9 us -> 0 us
  Pallas kernels: 73.9 us -> 85.2 us
    dot_general x3 -> x0, matrix products: 18.5 us -> none  [the longest x1 7.69 us: body(): lax.dot_general(weighted, flat_modes, contract_last, preferred_element_ty...]
    dot_general x1 -> x0, local copies, waits for them, and re-layouts: 11.7 us -> none  [body(): lax.dot_general(weighted, flat_modes, contract_last, preferred_element_ty...]
    pallas_call x0 -> x1, Pallas kernels: none -> 11.2 us  [products(): pl.pallas_call(products_kernel, grid=(parts,), out_shape=(jax.ShapeDtypeS...]
    reshape x1 -> x0, local copies, waits for them, and re-layouts: 11.2 us -> none  [body(): flat_modes = mode_shapes.reshape(mode_count, -1)]
    convert_element_type x1 -> x0, other arithmetic: 7.9 us -> none  [body(): weighted = (mode_shapes.astype(jnp.float32) * lumped_mass[None, None]).as...]
    another operation x1 -> x0, other arithmetic: 7.9 us -> none
    unnamed x24 -> x22, local copies, waits for them, and re-layouts: 11.8 us -> 11.8 us
where the time goes in v2:
time: 98.2 us; the launch traced here: 97.7 us
  Pallas kernels  85.2 us (87%)
  local copies, waits for them, and re-layouts  11.8 us (12%)
    pallas_call x1, Pallas kernels, run_steps(): pl.pallas_call(functools.partial(steps_kernel, heights, plan), out_shape=...  29.8 us
    pallas_call x1, Pallas kernels, gram_total(): pl.pallas_call(functools.partial(gram_kernel, count, plan), out_shape=jax...  18.3 us
    pallas_call x1, Pallas kernels, solve(): pl.pallas_call(solve_kernel, out_shape=jax.ShapeDtypeStruct(projected.sha...  16.5 us
    unnamed x22, local copies, waits for them, and re-layouts  11.8 us
    pallas_call x1, Pallas kernels, products(): pl.pallas_call(products_kernel, grid=(parts,), out_shape=(jax.ShapeDtypeS...  11.2 us
    pallas_call x1, Pallas kernels, coords_total(): pl.pallas_call(functools.partial(coords_kernel, count, plan), out_shape=j...  9.27 us

profile of v2, /device:TPU:0, one launch (start us, length us, event | category | flops | bytes accessed | tf_op | source)
XLA Modules:
  0.0 97.7 jit_solution(16251713028416556589)
XLA Ops:
  0.6 0.8 copy.15.table_ref
  1.4 0.0 copy-start.1
  1.4 1.0 %copy-done.1 = f32[3,8,1,40,128]{4,3,2,1,0:T(8,128)S(1)} copy-done((f32[3,8,1,40,128]{4,3,2,1,0:T(8,128)S(1)}, f32[3,8,1,40,128]{4,3,2,1,0:T(8,128)}, u32[]{:S(2)}) %copy-start.1) | copy-done | bytes 491544
  2.4 0.0 copy-start.2
  2.4 1.0 %copy-done.2 = f32[3,8,1,40,128]{4,3,2,1,0:T(8,128)S(1)} copy-done((f32[3,8,1,40,128]{4,3,2,1,0:T(8,128)S(1)}, f32[3,8,1,40,128]{4,3,2,1,0:T(8,128)}, u32[]{:S(2)}) %copy-start.2) | copy-done | bytes 491544
  3.4 0.0 copy-start.3
  3.5 1.0 %copy-done.3 = s32[3,8,1,40,128]{4,3,2,1,0:T(8,128)S(1)} copy-done((s32[3,8,1,40,128]{4,3,2,1,0:T(8,128)S(1)}, s32[3,8,1,40,128]{4,3,2,1,0:T(8,128)}, u32[]{:S(2)}) %copy-start.3) | copy-done | bytes 491544
  4.5 0.0 copy-start.4
  4.5 0.7 copy-done.4
  5.2 0.0 copy-start.5
  5.2 0.8 copy-done.5
  6.0 0.0 copy-start.6
  6.0 0.8 copy-done.6
  6.9 0.0 copy-start.7
  6.9 0.7 copy-done.7
  7.5 29.8 %time_steps.1 = (f32[3,40,128]{2,1,0:T(8,128)S(1)}, f32[3,40,128]{2,1,0:T(8,128)S(1)}, f32[3,8,40,128]{3,2,1,0:T(8,128)S(1)}, f32[3,8,40,128]{3,2,1,0:T(8,128)S(1)}, bf16[4,3,40,128]{3,2,1,0:T(8,128)(2,1)S(1)}) custom-call(f32[3,40,128]{2,1,0:T(8,128)S(1)} %bitcast.34, f32[3,40,128]{2,1,0:T(8,128)S(1)} %bitcast.35, f32[40,128]{1,0:T(8,128)S(1)} %bitcast.32, ...), custom_call_target="tpu_custom_call" | custom-call | tf_op jit(solution)/shard_map/time_steps/pallas_call | solution.py:363
  37.4 0.0 copy-start
  37.4 1.5 %copy-done = bf16[60,3,1,40,128]{4,3,2,1,0:T(8,128)(2,1)S(1)} copy-done((bf16[60,3,1,40,128]{4,3,2,1,0:T(8,128)(2,1)S(1)}, bf16[60,3,1,40,128]{4,3,2,1,0:T(8,128)(2,1)}, u32[]{:S(2)}) %copy-start) | copy-done | bytes 1843224
  38.9 11.2 %products.1 = (f32[256,256]{1,0:T(8,128)S(1)}, f32[256,64]{1,0:T(8,128)S(1)}) custom-call(bf16[256,3,40,128]{3,2,1,0:T(8,128)(2,1)} %bitcast.38, f32[40,128]{1,0:T(8,128)S(1)} %bitcast.33, bf16[60,3,40,128]{3,2,1,0:T(8,128)(2,1)S(1)} %bitcast.23, bf16[4,3,40,128]{3,2,1,0:T(8,128)(2,1)S(1)} %get-tuple-element.16.recent_ref), custom_call_target="tpu_custom_call" | custom-call | tf_op jit(solution)/shard_map/products/pallas_call | solution.py:590
  50.1 18.3 %gram_sum.1 = f32[32,8,256]{2,1,0:T(8,128)S(1)} custom-call(f32[32,8,256]{2,1,0:T(8,128)S(1)} %bitcast.31), custom_call_target="tpu_custom_call" | custom-call | tf_op jit(solution)/shard_map/gram_sum/pallas_call | solution.py:435
  68.4 16.5 %solve.1 = f32[256,64]{1,0:T(8,128)S(1)} custom-call(f32[256,256]{1,0:T(8,128)S(1)} %bitcast.24, f32[256,64]{1,0:T(8,128)S(1)} %get-tuple-element.18.projected_ref), custom_call_target="tpu_custom_call" | custom-call | tf_op jit(solution)/shard_map/solve/pallas_call | solution.py:519
  85.0 9.3 %coords_sum.1 = f32[8,64]{1,0:T(8,128)S(1)} custom-call(f32[32,8,64]{2,1,0:T(8,128)S(1)} %bitcast.25), custom_call_target="tpu_custom_call" | custom-call | tf_op jit(solution)/shard_map/coords_sum/pallas_call | solution.py:476
  94.3 0.6 copy.25
  94.9 0.6 copy.26
  95.5 0.8 copy.27
  96.3 0.8 copy.28
  97.1 0.6 copy.29
Async XLA Ops:
  1.4 1.0 %copy-start.1 = (f32[3,8,1,40,128]{4,3,2,1,0:T(8,128)S(1)}, f32[3,8,1,40,128]{4,3,2,1,0:T(8,128)}, u32[]{:S(2)}) copy-start(f32[3,8,1,40,128]{4,3,2,1,0:T(8,128)} %param.13) | copy-start | bytes 1474564
  2.4 1.0 %copy-start.2 = (f32[3,8,1,40,128]{4,3,2,1,0:T(8,128)S(1)}, f32[3,8,1,40,128]{4,3,2,1,0:T(8,128)}, u32[]{:S(2)}) copy-start(f32[3,8,1,40,128]{4,3,2,1,0:T(8,128)} %param.14) | copy-start | bytes 1474564
  3.4 1.0 %copy-start.3 = (s32[3,8,1,40,128]{4,3,2,1,0:T(8,128)S(1)}, s32[3,8,1,40,128]{4,3,2,1,0:T(8,128)}, u32[]{:S(2)}) copy-start(s32[3,8,1,40,128]{4,3,2,1,0:T(8,128)} %param.15) | copy-start | bytes 1474564
  4.5 0.7 copy-start.4
  5.2 0.8 copy-start.5
  6.0 0.8 copy-start.6
  6.9 0.7 copy-start.7
  37.4 1.5 %copy-start = (bf16[60,3,1,40,128]{4,3,2,1,0:T(8,128)(2,1)S(1)}, bf16[60,3,1,40,128]{4,3,2,1,0:T(8,128)(2,1)}, u32[]{:S(2)}) copy-start(bf16[60,3,1,40,128]{4,3,2,1,0:T(8,128)(2,1)} %param.18) | copy-start | bytes 5529604

commit v3 on v2

--- a/solution.py
+++ b/solution.py
@@ -74,11 +74,12 @@
 
 def steps_kernel(
     heights, plan,
-    disp_in, velo_in, mass_in, plastic_in, harden_in, ids_in, table_ref, accel_ref,
-    disp_out, velo_out, plastic_out, harden_out, snaps_out,
+    disp_in, velo_in, mass_in, plastic_in, harden_in, ids_in, table_ref, accel_ref, part_ref,
+    disp_out, velo_out, plastic_out, harden_out, snaps_out, gram_ref,
     velos, props, top_plastic, top_harden, top_ids, top_props,
     near_disp, near_velo, edge_send, edge_recv,
     disp_send_sem, disp_recv_sem, velo_send_sem, velo_recv_sem, state_send_sem, state_recv_sem,
+    landed, total, part_send_sem, part_recv_sem, give_sem, take_sem,
 ):
     h, p = lax.axis_index("height"), lax.axis_index("plan")
     fibres = plastic_in.shape[1]
@@ -93,18 +94,9 @@
     row = lax.broadcasted_iota(jnp.int32, (rows, columns), 0)
     last = columns - 1
 
-    barrier = pltpu.get_barrier_semaphore()
-
-    @pl.when(has_below)
-    def _():
-        signal(barrier, below)
-
-    @pl.when(has_above)
-    def _():
-        signal(barrier, above)
-
-    signal(barrier, left)
-    signal(barrier, right)
+    count = heights * plan
+    me = h * plan + p
+    barrier = greet_all(me, count, plan)
 
     velos[0] = velo_in[...]
     packed = [jnp.zeros((rows, columns), jnp.float32) for _ in range(3)]
@@ -116,8 +108,7 @@
     for part in range(3):
         edge_send[part] = packed[part]
 
-    greetings = 2 + has_below.astype(jnp.int32) + has_above.astype(jnp.int32)
-    pl.semaphore_wait(barrier, greetings)
+    pl.semaphore_wait(barrier, count - 1)
 
     def disp_copy(side, device):
         return remote(
@@ -186,6 +177,21 @@
     def _():
         for copy in state_copies():
             copy.start()
+
+    def send_part(offset, _):
+        target = lax.rem(me + offset, count)
+        remote(
+            part_ref.at[target], landed.at[offset - 1], part_send_sem, part_recv_sem,
+            mesh_id(target, plan),
+        ).start()
+        return 0
+
+    lax.fori_loop(1, count, send_part, 0)
+
+    def give_total(offset, _):
+        target = lax.rem(me + offset, count)
+        remote(total, gram_ref.at[me], give_sem, take_sem, mesh_id(target, plan)).start()
+        return 0
 
     @pl.when(jnp.logical_not(has_below))
     def _():
@@ -344,15 +350,23 @@
             for c in range(3):
                 velos[step + 1, c] = velo[c]
             exchange(step + 1, False)
+        if step == 0:
+            wait_bytes(landed, part_recv_sem)
+            total[...] = part_ref[me] + jnp.sum(landed[...], axis=0)
+            lax.fori_loop(1, count, give_total, 0)
+            gram_ref[me] = total[...]
         for c in range(3):
             disp[c] = disp[c] + time_step * velo[c]
             snaps_out[step, c] = disp[c].astype(jnp.bfloat16)
     for c in range(3):
         disp_out[c] = disp[c]
         velo_out[c] = velo[c]
-
-
-def run_steps(disp, velo, mass, plastic, harden, ids, table, accel):
+    wait_bytes(landed, take_sem)
+    wait_bytes(landed, part_send_sem)
+    wait_bytes(landed, give_sem)
+
+
+def run_steps(disp, velo, mass, plastic, harden, ids, table, accel, part):
     heights, plan = lax.axis_size("height"), lax.axis_size("plan")
     steps = accel.shape[0]
     vmem = pl.BlockSpec(memory_space=pltpu.VMEM)
@@ -360,7 +374,10 @@
     f32 = jnp.float32
     fibres = plastic.shape[1]
     plane = mass.shape
-    return pl.pallas_call(
+    count = heights * plan
+    modes = part.shape[0]
+    blocks = (count, modes // count, modes)
+    *ends, gram = pl.pallas_call(
         functools.partial(steps_kernel, heights, plan),
         out_shape=(
             jax.ShapeDtypeStruct(disp.shape, f32),
@@ -368,9 +385,10 @@
             jax.ShapeDtypeStruct(plastic.shape, f32),
             jax.ShapeDtypeStruct(harden.shape, f32),
             jax.ShapeDtypeStruct((steps,) + disp.shape, jnp.bfloat16),
+            jax.ShapeDtypeStruct(blocks, f32),
         ),
-        in_specs=[vmem] * 6 + [smem] * 2,
-        out_specs=(vmem,) * 5,
+        in_specs=[vmem] * 6 + [smem] * 2 + [vmem],
+        out_specs=(vmem,) * 6,
         scratch_shapes=[
             pltpu.VMEM((steps,) + velo.shape, f32),
             pltpu.VMEM((4,) + plastic.shape, f32),
@@ -388,65 +406,16 @@
             pltpu.SemaphoreType.DMA((steps, 4)),
             pltpu.SemaphoreType.DMA((4,)),
             pltpu.SemaphoreType.DMA((4,)),
-        ],
+            pltpu.VMEM((count - 1,) + blocks[1:], f32),
+            pltpu.VMEM(blocks[1:], f32),
+        ]
+        + [pltpu.SemaphoreType.DMA] * 4,
         compiler_params=pltpu.CompilerParams(
             collective_id=0, has_side_effects=True, vmem_limit_bytes=vmem_limit
         ),
         name="time_steps",
-    )(disp, velo, mass, plastic, harden, ids, table, accel)
-
-
-def gram_kernel(
-    count, plan, part_ref, out_ref, landed, total, send_sem, recv_sem, give_sem, take_sem
-):
-    me = lax.axis_index("height") * plan + lax.axis_index("plan")
-    barrier = greet_all(me, count, plan)
-    pl.semaphore_wait(barrier, count - 1)
-
-    def send(offset, _):
-        target = lax.rem(me + offset, count)
-        remote(
-            part_ref.at[target], landed.at[offset - 1], send_sem, recv_sem, mesh_id(target, plan)
-        ).start()
-        return 0
-
-    lax.fori_loop(1, count, send, 0)
-    wait_bytes(landed, recv_sem)
-    total[...] = part_ref[me] + jnp.sum(landed[...], axis=0)
-
-    def give(offset, _):
-        target = lax.rem(me + offset, count)
-        remote(total, out_ref.at[me], give_sem, take_sem, mesh_id(target, plan)).start()
-        return 0
-
-    lax.fori_loop(1, count, give, 0)
-    out_ref[me] = total[...]
-    wait_bytes(landed, take_sem)
-    wait_bytes(landed, send_sem)
-    wait_bytes(landed, give_sem)
-
-
-def gram_total(part):
-    plan = lax.axis_size("plan")
-    count = lax.axis_size(("height", "plan"))
-    modes = part.shape[0]
-    rows = modes // count
-    vmem = pl.BlockSpec(memory_space=pltpu.VMEM)
-    out = pl.pallas_call(
-        functools.partial(gram_kernel, count, plan),
-        out_shape=jax.ShapeDtypeStruct((count, rows, modes), jnp.float32),
-        in_specs=[vmem],
-        out_specs=vmem,
-        scratch_shapes=[
-            pltpu.VMEM((count - 1, rows, modes), jnp.float32),
-            pltpu.VMEM((rows, modes), jnp.float32),
-        ] + [pltpu.SemaphoreType.DMA] * 4,
-        compiler_params=pltpu.CompilerParams(
-            collective_id=1, has_side_effects=True, vmem_limit_bytes=vmem_limit
-        ),
-        name="gram_sum",
-    )(part.reshape(count, rows, modes))
-    return out.reshape(modes, modes)
+    )(disp, velo, mass, plastic, harden, ids, table, accel, part.reshape(blocks))
+    return *ends, gram.reshape(modes, modes)
 
 
 def coords_kernel(count, plan, part_ref, out_ref, landed, send_sem, recv_sem):
@@ -527,11 +496,10 @@
 
 
 def products_kernel(
-    modes_ref, mass_ref, history_ref, recent_ref, gram_ref, projected_ref, modes_wide, snaps_wide
+    modes_ref, mass_ref, history_ref, gram_ref, projected_ref, weighted_ref, modes_wide, snaps_wide
 ):
     modes, rows, columns = modes_ref.shape
-    earlier, recent = history_ref.shape[0], recent_ref.shape[0]
-    snaps = earlier + recent
+    earlier, snaps = history_ref.shape[0], projected_ref.shape[1]
     chunk = math.gcd(modes, 16)
     group = math.gcd(rows, 8)
 
@@ -549,8 +517,7 @@
         return 0
 
     lax.fori_loop(0, earlier, widen_history, 0)
-    for i in range(recent):
-        snaps_wide[pl.ds((earlier + i) * rows, rows), :] = recent_ref[i].astype(jnp.float32)
+    snaps_wide[earlier * rows :, :] = jnp.zeros(((snaps - earlier) * rows, columns), jnp.float32)
 
     @pl.when(pl.program_id(0) == 0)
     def _():
@@ -569,6 +536,7 @@
             plain.append(shape.astype(jnp.bfloat16))
             shots.append(snaps_wide[pl.ds(row, snaps, stride=rows), :].astype(jnp.bfloat16))
         left = jnp.concatenate(weighted, axis=1)
+        weighted_ref[i] = left
         gram_ref[...] += lax.dot_general(
             left, jnp.concatenate(plain, axis=1), contract_last,
             preferred_element_type=jnp.float32,
@@ -582,10 +550,11 @@
     lax.fori_loop(0, rows // group, add, 0)
 
 
-def products(mode_shapes, mass, history, recent):
+def products(mode_shapes, mass, history, snaps):
     modes, parts, rows, columns = mode_shapes.shape
-    earlier, later = history.shape[0], recent.shape[0]
-    snaps = earlier + later
+    earlier = history.shape[0]
+    group = math.gcd(rows, 8)
+    wide = (rows // group, modes, group * columns)
     f32 = jnp.float32
     return pl.pallas_call(
         products_kernel,
@@ -593,16 +562,17 @@
         out_shape=(
             jax.ShapeDtypeStruct((modes, modes), f32),
             jax.ShapeDtypeStruct((modes, snaps), f32),
+            jax.ShapeDtypeStruct((parts,) + wide, jnp.bfloat16),
         ),
         in_specs=[
             pl.BlockSpec((modes, None, rows, columns), lambda c: (0, c, 0, 0)),
             pl.BlockSpec((rows, columns), lambda c: (0, 0)),
             pl.BlockSpec((earlier, None, rows, columns), lambda c: (0, c, 0, 0)),
-            pl.BlockSpec((later, None, rows, columns), lambda c: (0, c, 0, 0)),
         ],
         out_specs=(
             pl.BlockSpec((modes, modes), lambda c: (0, 0)),
             pl.BlockSpec((modes, snaps), lambda c: (0, 0)),
+            pl.BlockSpec((None,) + wide, lambda c: (c, 0, 0, 0)),
         ),
         scratch_shapes=[
             pltpu.VMEM((modes * rows, columns), f32),
@@ -610,7 +580,52 @@
         ],
         compiler_params=pltpu.CompilerParams(vmem_limit_bytes=vmem_limit),
         name="products",
-    )(mode_shapes, mass, history, recent)
+    )(mode_shapes, mass, history)
+
+
+def recent_kernel(weighted_ref, recent_ref, before_ref, projected_ref, snaps_wide):
+    groups, modes, depth = weighted_ref.shape
+    recent, rows, columns = recent_ref.shape
+    snaps = projected_ref.shape[1]
+    earlier = snaps - recent
+    group = rows // groups
+
+    @pl.when(pl.program_id(0) == 0)
+    def _():
+        snaps_wide[: earlier * rows, :] = jnp.zeros((earlier * rows, columns), jnp.float32)
+        projected_ref[...] = before_ref[...]
+
+    for i in range(recent):
+        snaps_wide[pl.ds((earlier + i) * rows, rows), :] = recent_ref[i].astype(jnp.float32)
+    for i in range(groups):
+        shots = [
+            snaps_wide[pl.ds(i * group + j, snaps, stride=rows), :].astype(jnp.bfloat16)
+            for j in range(group)
+        ]
+        projected_ref[...] += lax.dot_general(
+            weighted_ref[i], jnp.concatenate(shots, axis=1), (((1,), (1,)), ((), ())),
+            preferred_element_type=jnp.float32,
+        )
+
+
+def add_recent(weighted, recent, before):
+    parts, groups, modes, depth = weighted.shape
+    later, _, rows, columns = recent.shape
+    snaps = before.shape[1]
+    return pl.pallas_call(
+        recent_kernel,
+        grid=(parts,),
+        out_shape=jax.ShapeDtypeStruct(before.shape, jnp.float32),
+        in_specs=[
+            pl.BlockSpec((None, groups, modes, depth), lambda c: (c, 0, 0, 0)),
+            pl.BlockSpec((later, None, rows, columns), lambda c: (0, c, 0, 0)),
+            pl.BlockSpec((modes, snaps), lambda c: (0, 0)),
+        ],
+        out_specs=pl.BlockSpec((modes, snaps), lambda c: (0, 0)),
+        scratch_shapes=[pltpu.VMEM((snaps * rows, columns), jnp.float32)],
+        compiler_params=pltpu.CompilerParams(vmem_limit_bytes=vmem_limit),
+        name="recent_products",
+    )(weighted, recent, before)
 
 
 def body(
@@ -625,14 +640,15 @@
     snapshot_history,
     mode_shapes,
 ):
-    disp_end, velo_end, plastic_end, harden_end, new_snaps = run_steps(
+    snaps = snapshot_history.shape[0] + ground_accel.shape[0]
+    mass_gram, projected, weighted = products(
+        mode_shapes[:, :, 0], lumped_mass[0], snapshot_history[:, :, 0], snaps
+    )
+    disp_end, velo_end, plastic_end, harden_end, new_snaps, gram = run_steps(
         displacement[:, 0], velocity[:, 0], lumped_mass[0], plastic_strain[:, :, 0],
-        hardening_strain[:, :, 0], material_ids[:, :, 0], material_table, ground_accel,
+        hardening_strain[:, :, 0], material_ids[:, :, 0], material_table, ground_accel, mass_gram,
     )
-    mass_gram, projected = products(
-        mode_shapes[:, :, 0], lumped_mass[0], snapshot_history[:, :, 0], new_snaps
-    )
-    gram = gram_total(mass_gram)
+    projected = add_recent(weighted, new_snaps, projected)
     modal_coords = coords_total(solve(gram, projected))
     return (
         disp_end[:, None], velo_end[:, None], plastic_end[:, :, None], harden_end[:, :, None],

time: 98.2 us -> 88.2 us (0.90)
  local copies, waits for them, and re-layouts: 11.8 us -> 6.41 us
  Pallas kernels: 85.2 us -> 80.8 us
    pallas_call x1, Pallas kernels: 18.3 us -> 5.3 us  [add_recent(): pl.pallas_call(recent_kernel, grid=(parts,), out_shape=jax.ShapeDtypeStru...]
    pallas_call x1, Pallas kernels: 29.8 us -> 37.6 us  [run_steps(): pl.pallas_call(functools.partial(steps_kernel, heights, plan), out_shape=...]
    unnamed x22, local copies, waits for them, and re-layouts: 11.8 us -> 6.41 us
    pallas_call x1, Pallas kernels: 11.2 us -> 13.6 us  [products(): pl.pallas_call(products_kernel, grid=(parts,), out_shape=(jax.ShapeDtypeS...]
    pallas_call x1, Pallas kernels: 9.27 us -> 7.81 us  [coords_total(): pl.pallas_call(functools.partial(coords_kernel, count, plan), out_shape=j...]
where the time goes in v3:
time: 88.2 us; the launch traced here: 87.9 us
  Pallas kernels  80.8 us (92%)
  local copies, waits for them, and re-layouts  6.41 us (7%)
    pallas_call x1, Pallas kernels, run_steps(): pl.pallas_call(functools.partial(steps_kernel, heights, plan), out_shape=...  37.6 us
    pallas_call x1, Pallas kernels, solve(): pl.pallas_call(solve_kernel, out_shape=jax.ShapeDtypeStruct(projected.sha...  16.5 us
    pallas_call x1, Pallas kernels, products(): pl.pallas_call(products_kernel, grid=(parts,), out_shape=(jax.ShapeDtypeS...  13.6 us
    pallas_call x1, Pallas kernels, coords_total(): pl.pallas_call(functools.partial(coords_kernel, count, plan), out_shape=j...  7.81 us
    unnamed x22, local copies, waits for them, and re-layouts  6.41 us
    pallas_call x1, Pallas kernels, add_recent(): pl.pallas_call(recent_kernel, grid=(parts,), out_shape=jax.ShapeDtypeStru...  5.3 us

profile of v3, /device:TPU:0, one launch (start us, length us, event | category | flops | bytes accessed | tf_op | source)
XLA Modules:
  0.0 87.9 jit_solution(18168687742429512880)
XLA Ops:
  0.6 0.0 copy-start.7
  0.6 0.8 copy.15.table_ref
  1.4 0.0 copy-start
  1.4 1.5 %copy-done = bf16[60,3,1,40,128]{4,3,2,1,0:T(8,128)(2,1)S(1)} copy-done((bf16[60,3,1,40,128]{4,3,2,1,0:T(8,128)(2,1)S(1)}, bf16[60,3,1,40,128]{4,3,2,1,0:T(8,128)(2,1)}, u32[]{:S(2)}) %copy-start) | copy-done | bytes 1843224
  2.9 0.0 copy-start.4
  2.9 0.7 copy-done.4
  3.6 0.0 copy-start.1
  3.6 0.0 copy-start.2
  3.6 0.0 copy-start.3
  3.6 0.0 copy-start.5
  3.6 0.0 copy-start.6
  3.7 13.6 %products.1 = (f32[256,256]{1,0:T(8,128)S(1)}, f32[256,64]{1,0:T(8,128)S(1)}, bf16[3,5,256,1024]{3,2,1,0:T(8,128)(2,1)}) custom-call(bf16[256,3,40,128]{3,2,1,0:T(8,128)(2,1)} %bitcast.38, f32[40,128]{1,0:T(8,128)S(1)} %bitcast.32, bf16[60,3,40,128]{3,2,1,0:T(8,128)(2,1)S(1)} %bitcast.23), custom_call_target="tpu_custom_call" | custom-call | tf_op jit(solution)/shard_map/products/pallas_call | solution.py:559
  17.2 0.0 copy-done.7
  17.2 0.0 copy-done.1
  17.2 0.0 copy-done.2
  17.2 0.0 copy-done.3
  17.2 0.0 copy-done.5
  17.3 0.0 copy-done.6
  17.3 37.6 %time_steps.1 = (f32[3,40,128]{2,1,0:T(8,128)S(1)}, f32[3,40,128]{2,1,0:T(8,128)S(1)}, f32[3,8,40,128]{3,2,1,0:T(8,128)S(1)}, f32[3,8,40,128]{3,2,1,0:T(8,128)S(...) custom-call(f32[3,40,128]{2,1,0:T(8,128)S(1)} %bitcast.34, f32[3,40,128]{2,1,0:T(8,128)S(1)} %bitcast.35, ...), custom_call_target="tpu_custom_call" | custom-call | tf_op jit(solution)/shard_map/time_steps/pallas_call | solution.py:380
  54.9 5.3 %recent_products.1.projected_ref = f32[256,64]{1,0:T(8,128)S(1)} custom-call(bf16[3,5,256,1024]{3,2,1,0:T(8,128)(2,1)} %get-tuple-element.20.weighted_ref, bf16[4,3,40,128]{3,2,1,0:T(8,128)(2,1)S(1)} %get-tuple-element.21.recent_ref, f32[256,64]{1,0:T(8,128)S(1)} %get-tuple-element.22.before_ref), custom_call_target="tpu_custom_call" | custom-call | tf_op jit(solution)/shard_map/recent_products/pallas_call | solution.py:615
  60.2 16.5 %solve.1 = f32[256,64]{1,0:T(8,128)S(1)} custom-call(f32[256,256]{1,0:T(8,128)S(1)} %bitcast.30, f32[256,64]{1,0:T(8,128)S(1)} %recent_products.1.projected_ref), custom_call_target="tpu_custom_call" | custom-call | tf_op jit(solution)/shard_map/solve/pallas_call | solution.py:488
  76.7 7.8 %coords_sum.1 = f32[8,64]{1,0:T(8,128)S(1)} custom-call(f32[32,8,64]{2,1,0:T(8,128)S(1)} %bitcast.24), custom_call_target="tpu_custom_call" | custom-call | tf_op jit(solution)/shard_map/coords_sum/pallas_call | solution.py:445
  84.5 0.6 copy.25
  85.2 0.6 copy.26
  85.8 0.8 copy.27
  86.6 0.8 copy.28
  87.4 0.6 copy.29
Async XLA Ops:
  0.6 16.6 %copy-start.7 = (f32[4,3]{1,0:T(4,128)S(1)}, f32[4,3]{1,0:T(4,128)}, u32[]{:S(2)}) copy-start(f32[4,3]{1,0:T(4,128)} %accel_ref.1) | copy-start | bytes 148
  1.4 1.5 %copy-start = (bf16[60,3,1,40,128]{4,3,2,1,0:T(8,128)(2,1)S(1)}, bf16[60,3,1,40,128]{4,3,2,1,0:T(8,128)(2,1)}, u32[]{:S(2)}) copy-start(bf16[60,3,1,40,128]{4,3,2,1,0:T(8,128)(2,1)} %param.18) | copy-start | bytes 5529604
  2.9 0.7 copy-start.4
  3.6 13.6 %copy-start.1 = (f32[3,8,1,40,128]{4,3,2,1,0:T(8,128)S(1)}, f32[3,8,1,40,128]{4,3,2,1,0:T(8,128)}, u32[]{:S(2)}) copy-start(f32[3,8,1,40,128]{4,3,2,1,0:T(8,128)} %param.13) | copy-start | bytes 1474564
  3.6 13.6 %copy-start.2 = (f32[3,8,1,40,128]{4,3,2,1,0:T(8,128)S(1)}, f32[3,8,1,40,128]{4,3,2,1,0:T(8,128)}, u32[]{:S(2)}) copy-start(f32[3,8,1,40,128]{4,3,2,1,0:T(8,128)} %param.14) | copy-start | bytes 1474564
  3.6 13.6 %copy-start.3 = (s32[3,8,1,40,128]{4,3,2,1,0:T(8,128)S(1)}, s32[3,8,1,40,128]{4,3,2,1,0:T(8,128)}, u32[]{:S(2)}) copy-start(s32[3,8,1,40,128]{4,3,2,1,0:T(8,128)} %param.15) | copy-start | bytes 1474564
  3.6 13.6 %copy-start.5 = (f32[3,1,40,128]{3,2,1,0:T(8,128)S(1)}, f32[3,1,40,128]{3,2,1,0:T(8,128)}, u32[]{:S(2)}) copy-start(f32[3,1,40,128]{3,2,1,0:T(8,128)} %param.10) | copy-start | bytes 184324
  3.6 13.6 %copy-start.6 = (f32[3,1,40,128]{3,2,1,0:T(8,128)S(1)}, f32[3,1,40,128]{3,2,1,0:T(8,128)}, u32[]{:S(2)}) copy-start(f32[3,1,40,128]{3,2,1,0:T(8,128)} %param.11) | copy-start | bytes 184324
